TPU v7x, 128 devices: a whole 4x4x4 slice. The times are simulated.
128 devices in a mesh: row: 4 (over x), col: 32 (over z, y, core).
Axes of the slice: x: 4, y: 4, z: 4, core: 2. Of those that a mesh axis runs over, the one named last changes fastest.
Arguments:
- shot_dose: float32 [4096, 128], P(('row', 'col')), may hold values from 0.5 to 1.5
- shot_frac: float32 [2, 4096, 128], P(None, ('row', 'col')), may hold values from 0 to 1
- shot_pos: int32 [4096, 128], P(('row', 'col')), may hold values from 0 to 262143
- block_count: int32 [4096], P(('row', 'col')), may hold values from 32 to 128, as said below
- shot_tile: int32 [4096, 1], P(('row', 'col')), may hold values from 0 to 31; in each aligned block of 32 rows (0 to 31, 32 to 63, ...) at most 2 rows name the same one
- zone: int32 [16, 512], P('row', 'col'), may hold values from 0 to 7
- zone_weights: float32 [8, 3], replicated, may hold values from 0.2 to 2
- target: float32 [1024, 32768], P('row', 'col'), may hold values from -0.6 to 0.6
Outputs:
- exposure: float32 [1024, 32768], P('row', 'col')
- shot_grad: float32 [4096, 128], P(('row', 'col'))
Inputs may be any that keep to these rules, and one draw needn't show every extreme that they name: block_count reaches 128 in at least one block of every device. `shot_tile`: within the 32 blocks of one device no tile column is named more than 2 times.
All inputs are finite; a program needn't handle non-finite values.
Results may differ from a plain program's by a relative error of at most 0.0001.
Values sent between devices are 32-bit elements; how exact they have to be, the bound alone decides.
A program may use at most 64 MiB of HBM per device.

v0:
```python
import functools
import math

import jax
import jax.numpy as jnp
import numpy as np
from jax import lax
from jax.experimental import pallas as pl
from jax.experimental.pallas import tpu as pltpu
from jax.sharding import PartitionSpec as P

HALO = 64
ZONES = 8
LANES = 128
CHUNK = 256
SIDE = 128
SIGMAS = (0.125 * HALO, 0.25 * HALO, 0.5 * HALO)
MESH = pl.DeviceIdType.MESH
F32, BF16, I32 = jnp.float32, jnp.bfloat16, jnp.int32


def iota(shape, dim):
    return lax.broadcasted_iota(I32, shape, dim)


def split(x):
    high = x.astype(BF16)
    return high, (x - high.astype(F32)).astype(BF16)


def dot(a, b):
    return jnp.dot(a, b, preferred_element_type=F32)


def dot_nt(a, b):
    return lax.dot_general(a, b, (((1,), (1,)), ((), ())), preferred_element_type=F32)


def pick(onehot, x):
    first = x.astype(BF16)
    rest = x - first.astype(F32)
    second = rest.astype(BF16)
    third = (rest - second.astype(F32)).astype(BF16)
    return dot(onehot, first) + dot(onehot, second) + dot(onehot, third)


def tap(offset, sigma):
    reach = np.arange(-HALO, HALO + 1).astype(np.float64)
    total = np.exp(-reach * reach / (2.0 * sigma * sigma)).sum()
    inside = np.abs(offset) <= HALO
    return np.where(inside, np.exp(-(offset.astype(np.float64) ** 2) / (2.0 * sigma * sigma)) / total, 0.0)


def halves(x):
    x = np.asarray(x, np.float32)
    high = x.astype(BF16)
    return high, (x - high.astype(np.float32)).astype(BF16)


def row_bands():
    i, y = np.arange(2 * HALO)[:, None], np.arange(4 * HALO)[None, :]
    return halves(np.concatenate([tap(y - HALO - i, sigma) for sigma in SIGMAS]))


def col_bands():
    x, c = np.arange(2 * CHUNK)[:, None], np.arange(CHUNK)[None, :]
    return halves(np.stack([tap(x - SIDE - c, sigma) for sigma in SIGMAS]))


def slots_of(tile, width):
    n = tile.shape[0]
    own, other = iota((n, width), 0), lax.rem(iota((n, width), 1), n)
    tile_row = jnp.sum(jnp.where(own == other, tile, 0), axis=0, keepdims=True)
    same = tile == tile_row
    rank_row = jnp.sum(jnp.where(same & (own < other), 1, 0), axis=0, keepdims=True)
    once = iota((n, width), 1) < n
    rank_col = jnp.sum(jnp.where(same & (other < own) & once, 1, 0), axis=1, keepdims=True)
    return tile * 2 + rank_col, tile_row * 2 + rank_row


def greet_all(n, me, row):
    barrier = pltpu.get_barrier_semaphore()

    def greet(step, carry):
        peer = lax.rem(me + step, n)
        pl.semaphore_signal(barrier, inc=1, device_id=(row, peer), device_id_type=MESH)
        return carry

    lax.fori_loop(1, n, greet, 0)
    return barrier


def exchange(n, me, row, source, target, send_sem, recv_sem):
    def copy_to(peer, slot):
        return pltpu.make_async_remote_copy(
            src_ref=source.at[peer],
            dst_ref=target.at[slot],
            send_sem=send_sem.at[peer],
            recv_sem=recv_sem.at[slot],
            device_id=(row, peer),
            device_id_type=MESH,
        )

    def start(step, carry):
        copy_to(lax.rem(me + step, n), me).start()
        return carry

    def finish(step, carry):
        peer = lax.rem(me + n - step, n)
        copy_to(peer, peer).wait_recv()
        return carry

    def drain(step, carry):
        copy_to(lax.rem(me + step, n), me).wait_send()
        return carry

    lax.fori_loop(1, n, start, 0)
    target[pl.ds(me, 1)] = source[pl.ds(me, 1)]
    lax.fori_loop(1, n, finish, 0)
    lax.fori_loop(1, n, drain, 0)


def route_kernel(n, dose, frac, pos, count, tile, recv, send, send_sem, recv_sem):
    row, me = lax.axis_index("row"), lax.axis_index("col")
    barrier = greet_all(n, me, row)
    blocks = tile.shape[0]
    _, placed = slots_of(tile[...], LANES)
    eye = iota((blocks, blocks), 0) == iota((blocks, blocks), 1)
    live_count = jnp.sum(jnp.where(eye, count[...], 0), axis=1, keepdims=True)
    live = iota((blocks, LANES), 1) < live_count
    amount = jnp.where(live, dose[...], 0.0)
    place = jnp.where(live, pos[...] + 1, 0).astype(F32)
    packed = jnp.concatenate([amount, frac[0], frac[1], place], axis=0)
    out, col = iota((8 * n, LANES), 0), iota((8 * n, LANES), 1)
    wanted = 2 * (out >> 3) + ((out >> 2) & 1)
    chosen = (wanted == placed) & ((out & 3) == lax.div(col, blocks))
    onehot = jnp.where(chosen, 1.0, 0.0).astype(BF16)
    send[...] = pick(onehot, packed).reshape(n, 8, LANES)
    pl.semaphore_wait(barrier, n - 1)
    exchange(n, me, row, send, recv, send_sem, recv_sem)


def route(n, dose, frac, pos, count, tile):
    vmem = pl.BlockSpec(memory_space=pltpu.VMEM)
    return pl.pallas_call(
        functools.partial(route_kernel, n),
        out_shape=jax.ShapeDtypeStruct((n, 8, LANES), F32),
        in_specs=[vmem] * 5,
        out_specs=vmem,
        scratch_shapes=[
            pltpu.VMEM((n, 8, LANES), F32),
            pltpu.SemaphoreType.DMA((n,)),
            pltpu.SemaphoreType.DMA((n,)),
        ],
        compiler_params=pltpu.CompilerParams(collective_id=0, has_side_effects=True),
        name="route",
    )(dose, frac, pos, count, tile)


def return_kernel(n, grads, tile, out, back, send_sem, recv_sem):
    row, me = lax.axis_index("row"), lax.axis_index("col")
    barrier = greet_all(n, me, row)
    blocks = tile.shape[0]
    placed, _ = slots_of(tile[...], LANES)
    col = iota((blocks, 8 * n), 1)
    chosen = (placed == 2 * (col >> 3) + (col & 7)) & ((col & 7) < 2)
    onehot = jnp.where(chosen, 1.0, 0.0).astype(BF16)
    pl.semaphore_wait(barrier, n - 1)
    exchange(n, me, row, grads, back, send_sem, recv_sem)
    out[...] = pick(onehot, back[...].reshape(8 * n, LANES))


def give_back(n, grads, tile):
    vmem = pl.BlockSpec(memory_space=pltpu.VMEM)
    return pl.pallas_call(
        functools.partial(return_kernel, n),
        out_shape=jax.ShapeDtypeStruct((tile.shape[0], LANES), F32),
        in_specs=[vmem] * 2,
        out_specs=vmem,
        scratch_shapes=[
            pltpu.VMEM((n, 8, LANES), F32),
            pltpu.SemaphoreType.DMA((n,)),
            pltpu.SemaphoreType.DMA((n,)),
        ],
        compiler_params=pltpu.CompilerParams(collective_id=2, has_side_effects=True),
        name="give_back",
    )(grads, tile)


def shot_rows(buf, chunk):
    both = [buf[2 * chunk], buf[2 * chunk + 1]]
    line = lambda f: jnp.concatenate([part[f : f + 1] for part in both], axis=1)
    place = line(3).astype(I32) - 1
    return line(0), line(1), line(2), place


def table(index, low, high, count):
    here = iota((count, index.shape[1]), 0).astype(F32).astype(BF16)
    first = index.astype(F32).astype(BF16)
    second = (index + 1).astype(F32).astype(BF16)
    at_first, at_second = here == first, here == second
    zero = jnp.zeros((), BF16)
    return [jnp.where(at_first, lo, jnp.where(at_second, hi, zero)) for lo, hi in zip(low, high)]


def col_tables(place, frac, cols):
    pixel = jnp.minimum(place & (cols - 1), cols - 2)
    low, high = split(1.0 - frac), split(frac)
    for begin in range(0, cols, LANES):
        local = jnp.clip(pixel - begin, -2, LANES)
        yield table(local, low, high, LANES)


def deposit_kernel(recv, dose, buf, counts, row_counts, sem):
    n = recv.shape[0]
    rows, cols = dose.shape
    shift = int(math.log2(cols))
    lane = iota((8, LANES), 1)
    places = recv[:, 3, :], recv[:, 7, :]
    live = [jnp.sum(jnp.where(place > 0.0, 1, 0), axis=1, keepdims=True) for place in places]
    which = iota((n, LANES), 1)
    spread = jnp.where(which < n, live[0], live[1])
    chosen = (lax.rem(which, n) == iota((n, LANES), 0)) & (which < 2 * n)
    row_counts[...] = jnp.sum(jnp.where(chosen, spread, 0), axis=0, keepdims=True)
    copy = pltpu.make_async_copy(row_counts, counts, sem)
    copy.start()
    dose[...] = jnp.zeros_like(dose)
    copy.wait()

    def place_block(block, amount, carry):
        at, current = carry
        lane_at, tile_at = at & (LANES - 1), at >> 7
        moved = pltpu.roll(block, lane_at, axis=1)
        merged = jnp.where(lane < lane_at, current, moved)
        buf[tile_at] = merged
        full = jnp.full((8, LANES), lane_at + amount, I32) >= LANES
        return at + amount, jnp.where(full, moved, merged)

    def compact(i, carry):
        block = recv[i]
        carry = place_block(block, counts[0, i], carry)
        return place_block(pltpu.roll(block, 4, axis=0), counts[0, n + i], carry)

    total, last = lax.fori_loop(0, n, compact, (jnp.int32(0), jnp.zeros((8, LANES), F32)))
    buf[total >> 7] = jnp.where(lane < (total & (LANES - 1)), last, 0.0)
    buf[(total >> 7) + 1] = jnp.zeros((8, LANES), F32)

    def deposit(chunk, carry):
        amount, frac_row, frac_col, place = shot_rows(buf, chunk)
        pixel_row = jnp.minimum(place >> shift, rows - 2)
        row_high, row_low = table(
            pixel_row, split(amount * (1.0 - frac_row)), split(amount * frac_row), rows
        )
        tables = list(col_tables(place, frac_col, cols))
        for begin in range(0, cols, CHUNK):
            part = tables[begin // LANES : (begin + CHUNK) // LANES]
            high = jnp.concatenate([t[0] for t in part], axis=0)
            low = jnp.concatenate([t[1] for t in part], axis=0)
            dose[:, begin : begin + CHUNK] += (
                dot_nt(row_high, high) + dot_nt(row_low, high) + dot_nt(row_high, low)
            )
        return carry

    lax.fori_loop(0, (total + CHUNK - 1) >> 8, deposit, 0)


def deposit(recv, rows, cols):
    vmem = pl.BlockSpec(memory_space=pltpu.VMEM)
    smem = pl.BlockSpec(memory_space=pltpu.SMEM)
    tiles = 2 * recv.shape[0] + 2
    return pl.pallas_call(
        deposit_kernel,
        out_shape=[
            jax.ShapeDtypeStruct((rows, cols), F32),
            jax.ShapeDtypeStruct((tiles, 8, LANES), F32),
            jax.ShapeDtypeStruct((1, LANES), I32),
        ],
        in_specs=[vmem],
        out_specs=[vmem, vmem, smem],
        scratch_shapes=[pltpu.VMEM((1, LANES), I32), pltpu.SemaphoreType.DMA],
        compiler_params=pltpu.CompilerParams(vmem_limit_bytes=32 * 2**20),
        name="deposit",
    )(recv)


def sample_kernel(grad_high, grad_low, buf, counts, out, values):
    n = out.shape[0]
    rows, cols = grad_high.shape
    shift = int(math.log2(cols))
    lane = iota((1, LANES), 1)
    total = lax.fori_loop(0, 2 * n, lambda i, t: t + counts[0, i], jnp.int32(0))

    def sample(chunk, carry):
        _, frac_row, frac_col, place = shot_rows(buf, chunk)
        pixel_row = jnp.minimum(place >> shift, rows - 2)
        tables = list(col_tables(place, frac_col, cols))
        high = jnp.concatenate([t[0] for t in tables], axis=0)
        low = jnp.concatenate([t[1] for t in tables], axis=0)
        along = dot(grad_high[...], high) + dot(grad_low[...], high) + dot(grad_high[...], low)
        here = iota((rows, CHUNK), 0)
        weight = jnp.where(
            here == pixel_row, 1.0 - frac_row, jnp.where(here == pixel_row + 1, frac_row, 0.0)
        )
        got = jnp.sum(weight * along, axis=0, keepdims=True)
        values[2 * chunk, 0:1] = got[:, :LANES]
        values[2 * chunk + 1, 0:1] = got[:, LANES:]
        return carry

    lax.fori_loop(0, (total + CHUNK - 1) >> 8, sample, 0)

    def take_block(amount, at):
        lane_at, tile_at = at & (LANES - 1), at >> 7
        both = jnp.where(lane >= lane_at, values[tile_at, 0:1], values[tile_at + 1, 0:1])
        moved = pltpu.roll(both, LANES - lane_at, axis=1)
        return jnp.where(lane < amount, moved, 0.0)

    row = iota((8, LANES), 0)

    def spread(i, at):
        first = take_block(counts[0, i], at)
        at = at + counts[0, i]
        second = take_block(counts[0, n + i], at)
        out[i] = jnp.where(row == 0, first, jnp.where(row == 1, second, 0.0))
        return at + counts[0, n + i]

    lax.fori_loop(0, n, spread, jnp.int32(0))


def sample(grad_high, grad_low, buf, counts):
    vmem = pl.BlockSpec(memory_space=pltpu.VMEM)
    smem = pl.BlockSpec(memory_space=pltpu.SMEM)
    n = (buf.shape[0] - 2) // 2
    return pl.pallas_call(
        sample_kernel,
        out_shape=jax.ShapeDtypeStruct((n, 8, LANES), F32),
        in_specs=[vmem, vmem, vmem, smem],
        out_specs=vmem,
        scratch_shapes=[pltpu.VMEM(buf.shape, F32)],
        compiler_params=pltpu.CompilerParams(vmem_limit_bytes=32 * 2**20),
        name="sample",
    )(grad_high, grad_low, buf, counts)


SIDES = ((-1, 0), (1, 0), (0, -1), (0, 1), (-1, -1), (-1, 1), (1, -1), (1, 1))


def blur_kernel(
    dims, dose, target, zone, zone_weights, row_high, row_low, col_high, col_low,
    exposure, grad_high, grad_low,
    zone_own, zone_in, halo_rows, halo_cols, halo_corners, dose_high, dose_low, part_high, part_low,
    error, weight, dose_send, dose_recv, error_send, error_recv, zone_send, zone_recv,
):
    n_row, n_col = dims
    rows, cols = dose.shape
    wide = cols + 2 * SIDE
    row, col = lax.axis_index("row"), lax.axis_index("col")

    def exists(side):
        down, right = SIDES[side]
        tests = []
        if down:
            tests.append(row > 0 if down < 0 else row < n_row - 1)
        if right:
            tests.append(col > 0 if right < 0 else col < n_col - 1)
        return functools.reduce(jnp.logical_and, tests)

    def neighbour(side):
        down, right = SIDES[side]
        return (row + down, col + right)

    def opposite(side):
        down, right = SIDES[side]
        return SIDES.index((-down, -right))

    def landing(turn, side):
        if side < 2:
            return halo_rows.at[turn, side]
        if side < 4:
            return halo_cols.at[turn, side - 2]
        return halo_corners.at[turn, side - 4]

    def edge(field, side):
        down, right = SIDES[side]
        high = slice(None) if not down else (pl.ds(0, HALO) if down < 0 else pl.ds(rows - HALO, HALO))
        across = slice(None) if not right else (pl.ds(0, SIDE) if right < 0 else pl.ds(cols - SIDE, SIDE))
        return field.at[high, across]

    def halo_copy(field, turn, side):
        sends, recvs = (dose_send, dose_recv) if turn == 0 else (error_send, error_recv)
        return pltpu.make_async_remote_copy(
            src_ref=edge(field, side),
            dst_ref=landing(turn, opposite(side)),
            send_sem=sends.at[side],
            recv_sem=recvs.at[opposite(side)],
            device_id=neighbour(side),
            device_id_type=MESH,
        )

    def zone_copy(side):
        return pltpu.make_async_remote_copy(
            src_ref=zone_own,
            dst_ref=zone_in.at[opposite(side)],
            send_sem=zone_send.at[side],
            recv_sem=zone_recv.at[opposite(side)],
            device_id=neighbour(side),
            device_id_type=MESH,
        )

    barrier = pltpu.get_barrier_semaphore()
    zone_own[...] = jnp.zeros_like(zone_own)
    zone_own[0 : zone.shape[0], 0 : zone.shape[1]] = zone[...]
    for side in range(8):

        @pl.when(jnp.logical_not(exists(side)))
        def _(side=side):
            for turn in range(2):
                spot = landing(turn, side)
                spot[...] = jnp.zeros_like(spot)
            zone_in[side] = jnp.zeros_like(zone_own)

    for side in range(8):

        @pl.when(exists(side))
        def _(side=side):
            pl.semaphore_signal(barrier, inc=1, device_id=neighbour(side), device_id_type=MESH)

    tall = 1 + jnp.where(row > 0, 1, 0) + jnp.where(row < n_row - 1, 1, 0)
    broad = 1 + jnp.where(col > 0, 1, 0) + jnp.where(col < n_col - 1, 1, 0)
    pl.semaphore_wait(barrier, tall * broad - 1)

    for side in range(8):

        @pl.when(exists(side))
        def _(side=side):
            halo_copy(dose, 0, side).start()
            zone_copy(side).start()

    def await_halo(field, turn, sides):
        for side in sides:

            @pl.when(exists(side))
            def _(side=side):
                halo_copy(field, turn, opposite(side)).wait_recv()

    def put_dose(value, first_row, first_col):
        high, low = split(value)
        here = pl.ds(first_row, value.shape[0]), pl.ds(first_col, value.shape[1])
        dose_high[here] = high
        dose_low[here] = low

    def along_cols(field, kernel):
        count = field.shape[0]
        stacked = [
            jnp.concatenate([part[:, b : b + 2 * CHUNK] for b in range(0, cols, CHUNK)], axis=0)
            for part in split(field)
        ]
        high, low = stacked
        out = (
            dot(high, col_high[kernel]) + dot(low, col_high[kernel]) + dot(high, col_low[kernel])
        )
        return jnp.concatenate(
            [out[i * count : (i + 1) * count] for i in range(cols // CHUNK)], axis=1
        )

    windows = {
        "top": (0, HALO, 0, 0),
        "mid": (HALO, 2 * HALO, HALO, 0),
        "low": (rows - HALO, HALO, 2 * HALO, HALO),
    }

    def row_blur(kernel, window, in_high, in_low):
        first, count, begin, band = windows[window]
        take = pl.ds(kernel * 2 * HALO + band, count)
        here = pl.ds(begin, 4 * HALO)
        high, low = row_high[take], row_low[take]
        return dot(high, in_high[here]) + dot(low, in_high[here]) + dot(high, in_low[here])

    def forward(window):
        first, count, _, _ = windows[window]
        total = [jnp.zeros((HALO, cols), F32) for _ in range(count // HALO)]
        for kernel in range(3):
            field = along_cols(row_blur(kernel, window, dose_high, dose_low), kernel)
            for i in range(count // HALO):
                square = 8 * kernel + 1 + first // HALO + i
                factor = weight[square : square + 1, SIDE : SIDE + cols]
                total[i] = total[i] + factor * field[i * HALO : (i + 1) * HALO]
        for i in range(count // HALO):
            here = pl.ds(first + i * HALO, HALO)
            exposure[here] = total[i]
            error[here] = total[i] - target[here]

    def put_part(value, first_row, first_col):
        across = pl.ds(first_col, value.shape[1])
        for i in range(value.shape[0] // HALO):
            square = first_row // HALO + i
            here = pl.ds(first_row + i * HALO, HALO)
            piece = value[i * HALO : (i + 1) * HALO]
            for kernel in range(3):
                factor = weight[8 * kernel + square : 8 * kernel + square + 1, across]
                high, low = split(factor * piece)
                part_high[kernel, here, across] = high
                part_low[kernel, here, across] = low

    def backward(window):
        first, count, _, _ = windows[window]
        total = jnp.zeros((count, cols), F32)
        for kernel in range(3):
            field = row_blur(kernel, window, part_high.at[kernel], part_low.at[kernel])
            total = total + along_cols(field, kernel)
        high, low = split(total)
        here = pl.ds(first, count)
        grad_high[here] = high
        grad_low[here] = low

    def zone_table():
        sub, lane = iota((8, LANES), 0), iota((8, LANES), 1)
        high, across = zone.shape
        own = pltpu.roll(pltpu.roll(zone_own[...], 1, axis=0), 2, axis=1)
        table = own
        for side in range(8):
            down, right = SIDES[side]
            got = zone_in[side]
            got = pltpu.roll(got, (1 + down * high) % 8, axis=0)
            got = pltpu.roll(got, (2 + right * across) % LANES, axis=1)
            row_ok = (sub == 0) if down < 0 else (sub == high + 1) if down > 0 else (sub >= 1) & (sub <= high)
            col_ok = (
                (lane == 1) if right < 0 else (lane == across + 2) if right > 0 else (lane >= 2) & (lane < across + 2)
            )
            table = jnp.where(row_ok & col_ok, got, table)
        picked = []
        for kernel in range(3):
            value = jnp.zeros((8, LANES), F32)
            for z in range(ZONES):
                value = jnp.where(table == z, zone_weights[z, kernel], value)
            picked.append(value)
        spread = iota((LANES, wide), 0) == iota((LANES, wide), 1) // HALO
        return picked, spread

    put_dose(dose[...], HALO, SIDE)
    for side in range(8):

        @pl.when(exists(side))
        def _(side=side):
            zone_copy(opposite(side)).wait_recv()

    picked, spread = zone_table()
    spread = jnp.where(spread, 1.0, 0.0).astype(BF16)
    stacked = jnp.concatenate(picked, axis=0)
    first_part = stacked.astype(BF16)
    rest = stacked - first_part.astype(F32)
    second_part = rest.astype(BF16)
    third_part = (rest - second_part.astype(F32)).astype(BF16)
    weight[...] = dot(first_part, spread) + dot(second_part, spread) + dot(third_part, spread)

    await_halo(dose, 0, (2, 3))
    put_dose(halo_cols[0, 0], HALO, 0)
    put_dose(halo_cols[0, 1], HALO, SIDE + cols)
    forward("mid")
    await_halo(dose, 0, (0, 1, 4, 5, 6, 7))
    for place, first_row in ((0, 0), (1, HALO + rows)):
        put_dose(halo_rows[0, place], first_row, SIDE)
        put_dose(halo_corners[0, 2 * place], first_row, 0)
        put_dose(halo_corners[0, 2 * place + 1], first_row, SIDE + cols)
    forward("top")
    forward("low")
    for side in range(8):

        @pl.when(exists(side))
        def _(side=side):
            halo_copy(error, 1, side).start()

    put_part(error[...], HALO, SIDE)
    await_halo(error, 1, (2, 3))
    put_part(halo_cols[1, 0], HALO, 0)
    put_part(halo_cols[1, 1], HALO, SIDE + cols)
    backward("mid")
    await_halo(error, 1, (0, 1, 4, 5, 6, 7))
    for place, first_row in ((0, 0), (1, HALO + rows)):
        put_part(halo_rows[1, place], first_row, SIDE)
        put_part(halo_corners[1, 2 * place], first_row, 0)
        put_part(halo_corners[1, 2 * place + 1], first_row, SIDE + cols)
    backward("top")
    backward("low")
    for side in range(8):

        @pl.when(exists(side))
        def _(side=side):
            halo_copy(dose, 0, side).wait_send()
            halo_copy(error, 1, side).wait_send()
            zone_copy(side).wait_send()


def blur(dims, dose, target, zone, zone_weights):
    rows, cols = dose.shape
    wide, high = cols + 2 * SIDE, rows + 2 * HALO
    vmem = pl.BlockSpec(memory_space=pltpu.VMEM)
    smem = pl.BlockSpec(memory_space=pltpu.SMEM)
    dma = pltpu.SemaphoreType.DMA((8,))
    return pl.pallas_call(
        functools.partial(blur_kernel, dims),
        out_shape=[
            jax.ShapeDtypeStruct((rows, cols), F32),
            jax.ShapeDtypeStruct((rows, cols), BF16),
            jax.ShapeDtypeStruct((rows, cols), BF16),
        ],
        in_specs=[vmem, vmem, vmem, smem, vmem, vmem, vmem, vmem],
        out_specs=[vmem] * 3,
        scratch_shapes=[
            pltpu.VMEM((8, LANES), I32),
            pltpu.VMEM((8, 8, LANES), I32),
            pltpu.VMEM((2, 2, HALO, cols), F32),
            pltpu.VMEM((2, 2, rows, SIDE), F32),
            pltpu.VMEM((2, 4, HALO, SIDE), F32),
            pltpu.VMEM((high, wide), BF16),
            pltpu.VMEM((high, wide), BF16),
            pltpu.VMEM((3, high, wide), BF16),
            pltpu.VMEM((3, high, wide), BF16),
            pltpu.VMEM((rows, cols), F32),
            pltpu.VMEM((24, wide), F32),
            dma, dma, dma, dma, dma, dma,
        ],
        compiler_params=pltpu.CompilerParams(
            collective_id=1, has_side_effects=True, vmem_limit_bytes=48 * 2**20
        ),
        name="blur",
    )(dose, target, zone, zone_weights, *row_bands(), *col_bands())


def per_device(dims, shot_dose, shot_frac, shot_pos, block_count, shot_tile, zone, zone_weights, target):
    n = dims[1]
    rows, cols = target.shape
    recv = route(n, shot_dose, shot_frac, shot_pos, block_count.reshape(1, -1), shot_tile)
    dose, buf, counts = deposit(recv, rows, cols)
    exposure, grad_high, grad_low = blur(dims, dose, target, zone, zone_weights)
    slot_grad = sample(grad_high, grad_low, buf, counts)
    return exposure, give_back(n, slot_grad, shot_tile)


def solution(mesh):
    dims = (mesh.shape["row"], mesh.shape["col"])
    return jax.shard_map(
        functools.partial(per_device, dims),
        mesh=mesh,
        in_specs=(
            P(("row", "col"), None),
            P(None, ("row", "col"), None),
            P(("row", "col"), None),
            P(("row", "col")),
            P(("row", "col"), None),
            P("row", "col"),
            P(),
            P("row", "col"),
        ),
        out_specs=(P("row", "col"), P(("row", "col"), None)),
        check_vma=False,
    )
```

profile of v0, /device:TPU:1, one launch (start us, length us, event | category | flops | bytes accessed | tf_op | source)
XLA Modules:
  0.0 103.4 jit_solution(8524156355919857126)
XLA Ops:
  0.6 0.0 copy-start.5
  0.6 0.8 copy.15.zone_weights
  1.4 1.3 %copy.14.tile = s32[32,1]{1,0:T(8,128)} copy(s32[32,1]{0,1:T(1,128)} %param.16) | data formatting | bytes 256 | tf_op args[4]
  2.8 14.5 %route.1.recv = f32[32,8,128]{2,1,0:T(8,128)} custom-call(f32[32,128]{1,0:T(8,128)} %dose.1, f32[2,32,128]{2,1,0:T(8,128)} %frac.1, s32[32,128]{1,0:T(8,128)} %pos.1, s32[1,32]{1,0:T(1,128)} %bitcast.1, s32[32,1]{1,0:T(8,128)} %copy.14.tile), custom_call_target="tpu_custom_call" | custom-call | tf_op jit(solution)/shard_map/route/pallas_call | solution.py:145
  17.3 0.0 copy-start.3
  17.3 0.9 copy-done.3
  18.2 8.7 %deposit.1 = (f32[256,1024]{1,0:T(8,128)S(1)}, f32[66,8,128]{2,1,0:T(8,128)S(1)}, s32[1,128]{1,0:T(1,128)S(1)}) custom-call(f32[32,8,128]{2,1,0:T(8,128)S(1)} %copy-done.3), custom_call_target="tpu_custom_call" | custom-call | tf_op jit(solution)/shard_map/deposit/pallas_call | solution.py:271
  26.9 0.0 copy-start.7
  26.9 0.0 copy-done.5
  26.9 0.7 copy-done.7
  27.6 0.0 copy-start
  27.6 1.2 %copy-done = f32[256,1024]{1,0:T(8,128)S(1)} copy-done((f32[256,1024]{1,0:T(8,128)S(1)}, f32[256,1024]{1,0:T(8,128)}, u32[]{:S(2)}) %copy-start) | copy-done | bytes 1048600
  28.8 0.0 copy-start.1
  28.8 1.1 %copy-done.1 = bf16[3,512,256]{2,1,0:T(8,128)(2,1)S(1)} copy-done((bf16[3,512,256]{2,1,0:T(8,128)(2,1)S(1)}, bf16[3,512,256]{2,1,0:T(8,128)(2,1)}, u32[]{:S(2)}) %copy-start.1) | copy-done | bytes 786456
  29.9 0.0 copy-start.2
  29.9 1.1 %copy-done.2 = bf16[3,512,256]{2,1,0:T(8,128)(2,1)S(1)} copy-done((bf16[3,512,256]{2,1,0:T(8,128)(2,1)S(1)}, bf16[3,512,256]{2,1,0:T(8,128)(2,1)}, u32[]{:S(2)}) %copy-start.2) | copy-done | bytes 786456
  31.0 0.0 copy-start.6
  31.0 0.9 copy-done.6
  32.0 34.1 %blur.1 = (f32[256,1024]{1,0:T(8,128)S(1)}, bf16[256,1024]{1,0:T(8,128)(2,1)S(1)}, bf16[256,1024]{1,0:T(8,128)(2,1)S(1)}) custom-call(f32[256,1024]{1,0:T(8,128)S(1)} %get-tuple-element.8.dose, f32[256,1024]{1,0:T(8,128)S(1)} %copy-done, s32[4,16]{1,0:T(4,128)S(1)} %copy-done.7, f32[8,3]{1,0:T(8,128)S(1)} %copy.15.zone_weights, ...), custom_call_target="tpu_custom_call" | custom-call | tf_op jit(solution)/shard_map/blur/pallas_call | solution.py:599
  66.1 8.4 %sample.1.grads = f32[32,8,128]{2,1,0:T(8,128)S(1)} custom-call(bf16[256,1024]{1,0:T(8,128)(2,1)S(1)} %get-tuple-element.10.grad_high, bf16[256,1024]{1,0:T(8,128)(2,1)S(1)} %get-tuple-element.11.grad_low, f32[66,8,128]{2,1,0:T(8,128)S(1)} %get-tuple-element.12.buf, s32[1,128]{1,0:T(1,128)S(1)} %get-tuple-element.13.counts), custom_call_target="tpu_custom_call" | custom-call | tf_op jit(solution)/shard_map/sample/pallas_call | solution.py:333
  74.5 0.0 copy-start.4
  74.5 0.7 copy-done.4
  75.2 26.6 %give_back.1 = f32[32,128]{1,0:T(8,128)} custom-call(f32[32,8,128]{2,1,0:T(8,128)} %copy-done.4, s32[32,1]{1,0:T(8,128)} %copy.14.tile), custom_call_target="tpu_custom_call" | custom-call | tf_op jit(solution)/shard_map/give_back/pallas_call | solution.py:175
  101.8 0.0 copy-start.8
  101.9 1.0 copy.19
  102.8 0.0 copy-done.8
  102.8 0.6 copy.20
Async XLA Ops:
  0.6 26.3 %copy-start.5 = (bf16[384,256]{1,0:T(8,128)(2,1)S(1)}, bf16[384,256]{1,0:T(8,128)(2,1)}, u32[]{:S(2)}) copy-start(bf16[384,256]{1,0:T(8,128)(2,1)} %constant.9.clone.row_low) | copy-start | bytes 589828
  17.3 0.9 copy-start.3
  26.9 0.7 copy-start.7
  27.6 1.2 %copy-start = (f32[256,1024]{1,0:T(8,128)S(1)}, f32[256,1024]{1,0:T(8,128)}, u32[]{:S(2)}) copy-start(f32[256,1024]{1,0:T(8,128)} %target.1) | copy-start | bytes 3145732
  28.8 1.1 %copy-start.1 = (bf16[3,512,256]{2,1,0:T(8,128)(2,1)S(1)}, bf16[3,512,256]{2,1,0:T(8,128)(2,1)}, u32[]{:S(2)}) copy-start(bf16[3,512,256]{2,1,0:T(8,128)(2,1)} %constant.11.clone.col_low) | copy-start | bytes 2359300
  29.9 1.1 %copy-start.2 = (bf16[3,512,256]{2,1,0:T(8,128)(2,1)S(1)}, bf16[3,512,256]{2,1,0:T(8,128)(2,1)}, u32[]{:S(2)}) copy-start(bf16[3,512,256]{2,1,0:T(8,128)(2,1)} %constant.10.clone.col_high) | copy-start | bytes 2359300
  31.0 0.9 copy-start.6
  74.5 0.7 copy-start.4
  101.8 1.0 copy-start.8
where the time goes:
time: 104 us; the launch traced here: 103 us
  Pallas kernels  92.4 us (89%)
  local copies, waits for them, and re-layouts  10.4 us (10%)
    pallas_call x1, Pallas kernels, blur(): pl.pallas_call(functools.partial(blur_kernel, dims), out_shape=[jax.Shape...  34.1 us
    pallas_call x1, Pallas kernels, give_back(): pl.pallas_call(functools.partial(return_kernel, n), out_shape=jax.ShapeDt...  26.6 us
    pallas_call x1, Pallas kernels, route(): pl.pallas_call(functools.partial(route_kernel, n), out_shape=jax.ShapeDty...  14.5 us
    unnamed x22, local copies, waits for them, and re-layouts  10.4 us
    pallas_call x1, Pallas kernels, deposit(): pl.pallas_call(deposit_kernel, out_shape=[jax.ShapeDtypeStruct((rows, col...  8.69 us
    pallas_call x1, Pallas kernels, sample(): pl.pallas_call(sample_kernel, out_shape=jax.ShapeDtypeStruct((n, 8, LANES...  8.44 us

commit v1 on v0

--- a/solution.py
+++ b/solution.py
@@ -19,6 +19,10 @@
 F32, BF16, I32 = jnp.float32, jnp.bfloat16, jnp.int32
 
 
+def cost(us):
+    return pl.CostEstimate(flops=0, bytes_accessed=int(us * 3.0e6), transcendentals=0)
+
+
 def iota(shape, dim):
     return lax.broadcasted_iota(I32, shape, dim)
 
@@ -69,13 +73,24 @@
 
 def slots_of(tile, width):
     n = tile.shape[0]
-    own, other = iota((n, width), 0), lax.rem(iota((n, width), 1), n)
+    times = width // n
+    own, lane = iota((n, width), 0), iota((n, width), 1)
+    other = lane // times
     tile_row = jnp.sum(jnp.where(own == other, tile, 0), axis=0, keepdims=True)
     same = tile == tile_row
     rank_row = jnp.sum(jnp.where(same & (own < other), 1, 0), axis=0, keepdims=True)
-    once = iota((n, width), 1) < n
+    once = lane % times == 0
     rank_col = jnp.sum(jnp.where(same & (other < own) & once, 1, 0), axis=1, keepdims=True)
     return tile * 2 + rank_col, tile_row * 2 + rank_row
+
+
+def upright(line):
+    n = line.shape[1]
+    return jnp.sum(jnp.where(iota((n, n), 0) == iota((n, n), 1), line, 0), axis=1, keepdims=True)
+
+
+def column_class(pixel):
+    return 2 * (pixel >> 8) + jnp.where((pixel & (CHUNK - 1)) == CHUNK - 1, 1, 0)
 
 
 def greet_all(n, me, row):
@@ -120,78 +135,116 @@
     lax.fori_loop(1, n, drain, 0)
 
 
-def route_kernel(n, dose, frac, pos, count, tile, recv, send, send_sem, recv_sem):
+def route_kernel(
+    n, cols, dose, frac, pos, count, tile, recv, order, parts, ordered, send, send_sem, recv_sem
+):
     row, me = lax.axis_index("row"), lax.axis_index("col")
     barrier = greet_all(n, me, row)
-    blocks = tile.shape[0]
-    _, placed = slots_of(tile[...], LANES)
-    eye = iota((blocks, blocks), 0) == iota((blocks, blocks), 1)
-    live_count = jnp.sum(jnp.where(eye, count[...], 0), axis=1, keepdims=True)
-    live = iota((blocks, LANES), 1) < live_count
-    amount = jnp.where(live, dose[...], 0.0)
-    place = jnp.where(live, pos[...] + 1, 0).astype(F32)
-    packed = jnp.concatenate([amount, frac[0], frac[1], place], axis=0)
-    out, col = iota((8 * n, LANES), 0), iota((8 * n, LANES), 1)
-    wanted = 2 * (out >> 3) + ((out >> 2) & 1)
-    chosen = (wanted == placed) & ((out & 3) == lax.div(col, blocks))
+    blocks = tile.shape[1]
+    live = iota((blocks, LANES), 1) < upright(count[...])
+    dead = 2 * (cols // CHUNK) - 1
+    kind = jnp.where(live, column_class(jnp.minimum(pos[...] & (cols - 1), cols - 2)), dead)
+    masks = [jnp.where(kind == j, 1.0, 0.0) for j in range(dead + 1)]
+    before = jnp.where(iota((LANES, LANES), 0) < iota((LANES, LANES), 1), 1.0, 0.0).astype(BF16)
+    prefix = dot(jnp.concatenate(masks, axis=0).astype(BF16), before)
+    start = jnp.zeros((blocks, 1), F32)
+    rank = jnp.zeros((blocks, LANES), F32)
+    for j, mask in enumerate(masks):
+        rank = rank + mask * (prefix[j * blocks : (j + 1) * blocks] + start)
+        start = start + jnp.sum(mask, axis=1, keepdims=True)
+    rank = rank.astype(I32)
+    order[...] = rank
+    fields = [
+        jnp.where(live, dose[...], 0.0),
+        frac[0],
+        frac[1],
+        jnp.where(live, pos[...] + 1, 0).astype(F32),
+    ]
+    for f, field in enumerate(fields):
+        for part in range(3):
+            piece = field.astype(BF16).astype(F32)
+            parts[:, 4 * part + f] = piece
+            field = field - piece
+        parts[:, 12 + f] = jnp.zeros((blocks, LANES), F32)
+    target = iota((LANES, LANES), 0)
+    for b in range(blocks):
+        moves = jnp.where(target == rank[b : b + 1], 1.0, 0.0).astype(BF16)
+        ordered[b] = dot_nt(parts[b].astype(BF16), moves)
+    width = 16 * blocks
+    _, placed = slots_of(upright(tile[...]), width)
+    out, col = iota((8 * n, width), 0), iota((8 * n, width), 1)
+    chosen = (out // 4 == placed) & (out % 4 == col % 4) & (col % 16 < 12)
     onehot = jnp.where(chosen, 1.0, 0.0).astype(BF16)
-    send[...] = pick(onehot, packed).reshape(n, 8, LANES)
+    send[...] = dot(onehot, ordered[...].reshape(width, LANES).astype(BF16)).reshape(n, 8, LANES)
     pl.semaphore_wait(barrier, n - 1)
     exchange(n, me, row, send, recv, send_sem, recv_sem)
 
 
-def route(n, dose, frac, pos, count, tile):
+def route(n, cols, dose, frac, pos, count, tile):
+    vmem = pl.BlockSpec(memory_space=pltpu.VMEM)
+    blocks = tile.shape[1]
+    return pl.pallas_call(
+        functools.partial(route_kernel, n, cols),
+        out_shape=[
+            jax.ShapeDtypeStruct((n, 8, LANES), F32),
+            jax.ShapeDtypeStruct((blocks, LANES), I32),
+        ],
+        in_specs=[vmem] * 5,
+        out_specs=[vmem] * 2,
+        scratch_shapes=[
+            pltpu.VMEM((blocks, 16, LANES), F32),
+            pltpu.VMEM((blocks, 16, LANES), F32),
+            pltpu.VMEM((n, 8, LANES), F32),
+            pltpu.SemaphoreType.DMA((n,)),
+            pltpu.SemaphoreType.DMA((n,)),
+        ],
+        compiler_params=pltpu.CompilerParams(
+            collective_id=0, has_side_effects=True, vmem_limit_bytes=8 * 2**20
+        ),
+        cost_estimate=cost(10),
+        name="route",
+    )(dose, frac, pos, count, tile)
+
+
+def return_kernel(n, grads, tile, order, out, back, send_sem, recv_sem):
+    row, me = lax.axis_index("row"), lax.axis_index("col")
+    barrier = greet_all(n, me, row)
+    blocks = tile.shape[1]
+    placed, _ = slots_of(upright(tile[...]), blocks)
+    col = iota((blocks, 8 * n), 1)
+    chosen = (placed == 2 * (col >> 3) + (col & 7)) & ((col & 7) < 2)
+    onehot = jnp.where(chosen, 1.0, 0.0).astype(BF16)
+    pl.semaphore_wait(barrier, n - 1)
+    exchange(n, me, row, grads, back, send_sem, recv_sem)
+    found = pick(onehot, back[...].reshape(8 * n, LANES))
+    out[...] = jnp.take_along_axis(found, order[...], axis=1)
+
+
+def give_back(n, grads, tile, order):
     vmem = pl.BlockSpec(memory_space=pltpu.VMEM)
     return pl.pallas_call(
-        functools.partial(route_kernel, n),
-        out_shape=jax.ShapeDtypeStruct((n, 8, LANES), F32),
-        in_specs=[vmem] * 5,
+        functools.partial(return_kernel, n),
+        out_shape=jax.ShapeDtypeStruct((tile.shape[1], LANES), F32),
+        in_specs=[vmem] * 3,
         out_specs=vmem,
         scratch_shapes=[
             pltpu.VMEM((n, 8, LANES), F32),
             pltpu.SemaphoreType.DMA((n,)),
             pltpu.SemaphoreType.DMA((n,)),
         ],
-        compiler_params=pltpu.CompilerParams(collective_id=0, has_side_effects=True),
-        name="route",
-    )(dose, frac, pos, count, tile)
-
-
-def return_kernel(n, grads, tile, out, back, send_sem, recv_sem):
-    row, me = lax.axis_index("row"), lax.axis_index("col")
-    barrier = greet_all(n, me, row)
-    blocks = tile.shape[0]
-    placed, _ = slots_of(tile[...], LANES)
-    col = iota((blocks, 8 * n), 1)
-    chosen = (placed == 2 * (col >> 3) + (col & 7)) & ((col & 7) < 2)
-    onehot = jnp.where(chosen, 1.0, 0.0).astype(BF16)
-    pl.semaphore_wait(barrier, n - 1)
-    exchange(n, me, row, grads, back, send_sem, recv_sem)
-    out[...] = pick(onehot, back[...].reshape(8 * n, LANES))
-
-
-def give_back(n, grads, tile):
-    vmem = pl.BlockSpec(memory_space=pltpu.VMEM)
-    return pl.pallas_call(
-        functools.partial(return_kernel, n),
-        out_shape=jax.ShapeDtypeStruct((tile.shape[0], LANES), F32),
-        in_specs=[vmem] * 2,
-        out_specs=vmem,
-        scratch_shapes=[
-            pltpu.VMEM((n, 8, LANES), F32),
-            pltpu.SemaphoreType.DMA((n,)),
-            pltpu.SemaphoreType.DMA((n,)),
-        ],
-        compiler_params=pltpu.CompilerParams(collective_id=2, has_side_effects=True),
+        compiler_params=pltpu.CompilerParams(
+            collective_id=2, has_side_effects=True, vmem_limit_bytes=8 * 2**20
+        ),
+        cost_estimate=cost(10),
         name="give_back",
-    )(grads, tile)
-
-
-def shot_rows(buf, chunk):
-    both = [buf[2 * chunk], buf[2 * chunk + 1]]
+    )(grads, tile, order)
+
+
+def shot_rows(buf, first, end):
+    lane = iota((8, LANES), 1)
+    both = [jnp.where(lane < end, buf[first], 0.0), jnp.where(lane < end - LANES, buf[first + 1], 0.0)]
     line = lambda f: jnp.concatenate([part[f : f + 1] for part in both], axis=1)
-    place = line(3).astype(I32) - 1
-    return line(0), line(1), line(2), place
+    return line(0), line(1), line(2), line(3).astype(I32) - 1
 
 
 def table(index, low, high, count):
@@ -203,150 +256,190 @@
     return [jnp.where(at_first, lo, jnp.where(at_second, hi, zero)) for lo, hi in zip(low, high)]
 
 
-def col_tables(place, frac, cols):
+def col_table(place, frac, cols, window):
     pixel = jnp.minimum(place & (cols - 1), cols - 2)
-    low, high = split(1.0 - frac), split(frac)
-    for begin in range(0, cols, LANES):
-        local = jnp.clip(pixel - begin, -2, LANES)
-        yield table(local, low, high, LANES)
-
-
-def deposit_kernel(recv, dose, buf, counts, row_counts, sem):
+    local = jnp.clip(pixel - window * CHUNK, -2, CHUNK)
+    return table(local, split(1.0 - frac), split(frac), CHUNK)
+
+
+def tiles_of_bin(n):
+    return 2 * n + 2
+
+
+def deposit_kernel(recv, dose, buf, spans, row_spans, sem):
     n = recv.shape[0]
     rows, cols = dose.shape
+    bins = cols // CHUNK
     shift = int(math.log2(cols))
     lane = iota((8, LANES), 1)
-    places = recv[:, 3, :], recv[:, 7, :]
-    live = [jnp.sum(jnp.where(place > 0.0, 1, 0), axis=1, keepdims=True) for place in places]
+    ends = []
+    for half in range(2):
+        place = recv[:, 4 * half + 3, :].astype(I32) - 1
+        kind = column_class(jnp.minimum(place & (cols - 1), cols - 2))
+        kind = jnp.where(place >= 0, kind, 2 * bins)
+        ends.append([jnp.sum(jnp.where(kind <= j, 1, 0), axis=1, keepdims=True) for j in range(2 * bins)])
     which = iota((n, LANES), 1)
-    spread = jnp.where(which < n, live[0], live[1])
     chosen = (lax.rem(which, n) == iota((n, LANES), 0)) & (which < 2 * n)
-    row_counts[...] = jnp.sum(jnp.where(chosen, spread, 0), axis=0, keepdims=True)
-    copy = pltpu.make_async_copy(row_counts, counts, sem)
+
+    def to_lanes(first, second):
+        spread = jnp.where(which < n, first, second)
+        return jnp.sum(jnp.where(chosen, spread, 0), axis=0, keepdims=True)
+
+    lines = []
+    for q in range(bins):
+        lines.append(to_lanes(*(e[2 * q - 2] if q else jnp.zeros((n, 1), I32) for e in ends)))
+    for q in range(bins):
+        lines.append(to_lanes(*(e[2 * q + 1] for e in ends)) - lines[q])
+    row_spans[...] = jnp.concatenate(lines, axis=0)
+    copy = pltpu.make_async_copy(row_spans, spans, sem)
     copy.start()
     dose[...] = jnp.zeros_like(dose)
     copy.wait()
 
-    def place_block(block, amount, carry):
+    def append(block, begin, amount, carry):
         at, current = carry
-        lane_at, tile_at = at & (LANES - 1), at >> 7
-        moved = pltpu.roll(block, lane_at, axis=1)
+        lane_at = at & (LANES - 1)
+        moved = pltpu.roll(block, (at - begin) & (LANES - 1), axis=1)
         merged = jnp.where(lane < lane_at, current, moved)
-        buf[tile_at] = merged
+        buf[at >> 7] = merged
         full = jnp.full((8, LANES), lane_at + amount, I32) >= LANES
         return at + amount, jnp.where(full, moved, merged)
 
-    def compact(i, carry):
+    def gather(i, carry):
         block = recv[i]
-        carry = place_block(block, counts[0, i], carry)
-        return place_block(pltpu.roll(block, 4, axis=0), counts[0, n + i], carry)
-
-    total, last = lax.fori_loop(0, n, compact, (jnp.int32(0), jnp.zeros((8, LANES), F32)))
-    buf[total >> 7] = jnp.where(lane < (total & (LANES - 1)), last, 0.0)
-    buf[(total >> 7) + 1] = jnp.zeros((8, LANES), F32)
+        for half in range(2):
+            index = half * n + i
+            carry = [
+                append(block, spans[q, index], spans[bins + q, index], carry[q]) for q in range(bins)
+            ]
+            block = pltpu.roll(block, 4, axis=0)
+        return carry
+
+    starts = [q * tiles_of_bin(n) for q in range(bins)]
+    empty = jnp.zeros((8, LANES), F32)
+    found = lax.fori_loop(0, n, gather, [(jnp.int32(s * LANES), empty) for s in starts])
+    most = jnp.int32(0)
+    for q, (at, last) in enumerate(found):
+        buf[at >> 7] = jnp.where(lane < (at & (LANES - 1)), last, 0.0)
+        buf[(at >> 7) + 1] = empty
+        most = jnp.maximum(most, (at - starts[q] * LANES + CHUNK - 1) >> 8)
+    spans[0, LANES - 1] = most
 
     def deposit(chunk, carry):
-        amount, frac_row, frac_col, place = shot_rows(buf, chunk)
-        pixel_row = jnp.minimum(place >> shift, rows - 2)
-        row_high, row_low = table(
-            pixel_row, split(amount * (1.0 - frac_row)), split(amount * frac_row), rows
-        )
-        tables = list(col_tables(place, frac_col, cols))
-        for begin in range(0, cols, CHUNK):
-            part = tables[begin // LANES : (begin + CHUNK) // LANES]
-            high = jnp.concatenate([t[0] for t in part], axis=0)
-            low = jnp.concatenate([t[1] for t in part], axis=0)
-            dose[:, begin : begin + CHUNK] += (
+        for q in range(bins):
+            first = starts[q] + 2 * chunk
+            end = found[q][0] - first * LANES
+            amount, frac_row, frac_col, place = shot_rows(buf, first, end)
+            pixel_row = jnp.minimum(place >> shift, rows - 2)
+            row_high, row_low = table(
+                pixel_row, split(amount * (1.0 - frac_row)), split(amount * frac_row), rows
+            )
+            high, low = col_table(place, frac_col, cols, q)
+            dose[:, q * CHUNK : (q + 1) * CHUNK] += (
                 dot_nt(row_high, high) + dot_nt(row_low, high) + dot_nt(row_high, low)
             )
         return carry
 
-    lax.fori_loop(0, (total + CHUNK - 1) >> 8, deposit, 0)
+    lax.fori_loop(0, most, deposit, 0)
 
 
 def deposit(recv, rows, cols):
     vmem = pl.BlockSpec(memory_space=pltpu.VMEM)
     smem = pl.BlockSpec(memory_space=pltpu.SMEM)
-    tiles = 2 * recv.shape[0] + 2
+    tiles = (cols // CHUNK) * tiles_of_bin(recv.shape[0])
+    spans = (2 * (cols // CHUNK), LANES)
     return pl.pallas_call(
         deposit_kernel,
         out_shape=[
             jax.ShapeDtypeStruct((rows, cols), F32),
             jax.ShapeDtypeStruct((tiles, 8, LANES), F32),
-            jax.ShapeDtypeStruct((1, LANES), I32),
+            jax.ShapeDtypeStruct(spans, I32),
         ],
         in_specs=[vmem],
         out_specs=[vmem, vmem, smem],
-        scratch_shapes=[pltpu.VMEM((1, LANES), I32), pltpu.SemaphoreType.DMA],
-        compiler_params=pltpu.CompilerParams(vmem_limit_bytes=32 * 2**20),
+        scratch_shapes=[pltpu.VMEM(spans, I32), pltpu.SemaphoreType.DMA],
+        compiler_params=pltpu.CompilerParams(vmem_limit_bytes=16 * 2**20),
+        cost_estimate=cost(8),
         name="deposit",
     )(recv)
 
 
-def sample_kernel(grad_high, grad_low, buf, counts, out, values):
+def sample_kernel(grad_high, grad_low, buf, spans, out, values):
     n = out.shape[0]
     rows, cols = grad_high.shape
+    bins = cols // CHUNK
     shift = int(math.log2(cols))
-    lane = iota((1, LANES), 1)
-    total = lax.fori_loop(0, 2 * n, lambda i, t: t + counts[0, i], jnp.int32(0))
+    starts = [q * tiles_of_bin(n) for q in range(bins)]
 
     def sample(chunk, carry):
-        _, frac_row, frac_col, place = shot_rows(buf, chunk)
-        pixel_row = jnp.minimum(place >> shift, rows - 2)
-        tables = list(col_tables(place, frac_col, cols))
-        high = jnp.concatenate([t[0] for t in tables], axis=0)
-        low = jnp.concatenate([t[1] for t in tables], axis=0)
-        along = dot(grad_high[...], high) + dot(grad_low[...], high) + dot(grad_high[...], low)
-        here = iota((rows, CHUNK), 0)
-        weight = jnp.where(
-            here == pixel_row, 1.0 - frac_row, jnp.where(here == pixel_row + 1, frac_row, 0.0)
-        )
-        got = jnp.sum(weight * along, axis=0, keepdims=True)
-        values[2 * chunk, 0:1] = got[:, :LANES]
-        values[2 * chunk + 1, 0:1] = got[:, LANES:]
+        for q in range(bins):
+            first = starts[q] + 2 * chunk
+            _, frac_row, frac_col, place = shot_rows(buf, first, CHUNK)
+            pixel_row = jnp.minimum(place >> shift, rows - 2)
+            high, low = col_table(place, frac_col, cols, q)
+            window = slice(q * CHUNK, (q + 1) * CHUNK)
+            along = (
+                dot(grad_high[:, window], high)
+                + dot(grad_low[:, window], high)
+                + dot(grad_high[:, window], low)
+            )
+            here = iota((rows, CHUNK), 0)
+            weight = jnp.where(
+                here == pixel_row, 1.0 - frac_row, jnp.where(here == pixel_row + 1, frac_row, 0.0)
+            )
+            got = jnp.sum(weight * along, axis=0, keepdims=True)
+            values[first, 0:1] = got[:, :LANES]
+            values[first + 1, 0:1] = got[:, LANES:]
         return carry
 
-    lax.fori_loop(0, (total + CHUNK - 1) >> 8, sample, 0)
-
-    def take_block(amount, at):
+    lax.fori_loop(0, spans[0, LANES - 1], sample, 0)
+
+    lane, row = iota((1, LANES), 1), iota((8, LANES), 0)
+
+    def take(begin, amount, at):
         lane_at, tile_at = at & (LANES - 1), at >> 7
         both = jnp.where(lane >= lane_at, values[tile_at, 0:1], values[tile_at + 1, 0:1])
-        moved = pltpu.roll(both, LANES - lane_at, axis=1)
-        return jnp.where(lane < amount, moved, 0.0)
-
-    row = iota((8, LANES), 0)
+        moved = pltpu.roll(both, (begin - at) & (LANES - 1), axis=1)
+        return jnp.where((lane >= begin) & (lane < begin + amount), moved, 0.0)
 
     def spread(i, at):
-        first = take_block(counts[0, i], at)
-        at = at + counts[0, i]
-        second = take_block(counts[0, n + i], at)
-        out[i] = jnp.where(row == 0, first, jnp.where(row == 1, second, 0.0))
-        return at + counts[0, n + i]
-
-    lax.fori_loop(0, n, spread, jnp.int32(0))
-
-
-def sample(grad_high, grad_low, buf, counts):
+        at = list(at)
+        both = []
+        for half in range(2):
+            total = jnp.zeros((1, LANES), F32)
+            for q in range(bins):
+                begin, amount = spans[q, half * n + i], spans[bins + q, half * n + i]
+                total = total + take(begin, amount, at[q])
+                at[q] = at[q] + amount
+            both.append(total)
+        out[i] = jnp.where(row == 0, both[0], jnp.where(row == 1, both[1], 0.0))
+        return at
+
+    lax.fori_loop(0, n, spread, [jnp.int32(s * LANES) for s in starts])
+
+
+def sample(n, grad_high, grad_low, buf, spans):
     vmem = pl.BlockSpec(memory_space=pltpu.VMEM)
     smem = pl.BlockSpec(memory_space=pltpu.SMEM)
-    n = (buf.shape[0] - 2) // 2
     return pl.pallas_call(
         sample_kernel,
         out_shape=jax.ShapeDtypeStruct((n, 8, LANES), F32),
         in_specs=[vmem, vmem, vmem, smem],
         out_specs=vmem,
         scratch_shapes=[pltpu.VMEM(buf.shape, F32)],
-        compiler_params=pltpu.CompilerParams(vmem_limit_bytes=32 * 2**20),
+        compiler_params=pltpu.CompilerParams(vmem_limit_bytes=16 * 2**20),
+        cost_estimate=cost(8),
         name="sample",
-    )(grad_high, grad_low, buf, counts)
+    )(grad_high, grad_low, buf, spans)
 
 
 SIDES = ((-1, 0), (1, 0), (0, -1), (0, 1), (-1, -1), (-1, 1), (1, -1), (1, 1))
 
 
 def blur_kernel(
-    dims, dose, target, zone, zone_weights, row_high, row_low, col_high, col_low,
+    dims, dose, target_far, zone, zone_weights, row_high_far, row_low_far, col_high_far, col_low_far,
     exposure, grad_high, grad_low,
+    target, row_high, row_low, col_high, col_low, near_sem,
     zone_own, zone_in, halo_rows, halo_cols, halo_corners, dose_high, dose_low, part_high, part_low,
     error, weight, dose_send, dose_recv, error_send, error_recv, zone_send, zone_recv,
 ):
@@ -406,6 +499,20 @@
             device_id_type=MESH,
         )
 
+    near = [
+        pltpu.make_async_copy(far, close, near_sem.at[i])
+        for i, (far, close) in enumerate(
+            (
+                (row_high_far, row_high),
+                (row_low_far, row_low),
+                (col_high_far, col_high),
+                (col_low_far, col_low),
+                (target_far, target),
+            )
+        )
+    ]
+    for copy in near:
+        copy.start()
     barrier = pltpu.get_barrier_semaphore()
     zone_own[...] = jnp.zeros_like(zone_own)
     zone_own[0 : zone.shape[0], 0 : zone.shape[1]] = zone[...]
@@ -531,7 +638,7 @@
         for kernel in range(3):
             value = jnp.zeros((8, LANES), F32)
             for z in range(ZONES):
-                value = jnp.where(table == z, zone_weights[z, kernel], value)
+                value = jnp.where(table == z, zone_weights[kernel, z], value)
             picked.append(value)
         spread = iota((LANES, wide), 0) == iota((LANES, wide), 1) // HALO
         return picked, spread
@@ -552,6 +659,8 @@
     third_part = (rest - second_part.astype(F32)).astype(BF16)
     weight[...] = dot(first_part, spread) + dot(second_part, spread) + dot(third_part, spread)
 
+    for copy in near:
+        copy.wait()
     await_halo(dose, 0, (2, 3))
     put_dose(halo_cols[0, 0], HALO, 0)
     put_dose(halo_cols[0, 1], HALO, SIDE + cols)
@@ -595,7 +704,9 @@
     wide, high = cols + 2 * SIDE, rows + 2 * HALO
     vmem = pl.BlockSpec(memory_space=pltpu.VMEM)
     smem = pl.BlockSpec(memory_space=pltpu.SMEM)
+    far = pl.BlockSpec(memory_space=pltpu.HBM)
     dma = pltpu.SemaphoreType.DMA((8,))
+    bands = (*row_bands(), *col_bands())
     return pl.pallas_call(
         functools.partial(blur_kernel, dims),
         out_shape=[
@@ -603,9 +714,12 @@
             jax.ShapeDtypeStruct((rows, cols), BF16),
             jax.ShapeDtypeStruct((rows, cols), BF16),
         ],
-        in_specs=[vmem, vmem, vmem, smem, vmem, vmem, vmem, vmem],
+        in_specs=[vmem, far, vmem, smem, far, far, far, far],
         out_specs=[vmem] * 3,
         scratch_shapes=[
+            pltpu.VMEM((rows, cols), F32),
+            *[pltpu.VMEM(band.shape, BF16) for band in bands],
+            pltpu.SemaphoreType.DMA((5,)),
             pltpu.VMEM((8, LANES), I32),
             pltpu.VMEM((8, 8, LANES), I32),
             pltpu.VMEM((2, 2, HALO, cols), F32),
@@ -620,20 +734,22 @@
             dma, dma, dma, dma, dma, dma,
         ],
         compiler_params=pltpu.CompilerParams(
-            collective_id=1, has_side_effects=True, vmem_limit_bytes=48 * 2**20
+            collective_id=1, has_side_effects=True, vmem_limit_bytes=32 * 2**20
         ),
+        cost_estimate=cost(25),
         name="blur",
-    )(dose, target, zone, zone_weights, *row_bands(), *col_bands())
+    )(dose, target, zone, zone_weights, *bands)
 
 
 def per_device(dims, shot_dose, shot_frac, shot_pos, block_count, shot_tile, zone, zone_weights, target):
     n = dims[1]
     rows, cols = target.shape
-    recv = route(n, shot_dose, shot_frac, shot_pos, block_count.reshape(1, -1), shot_tile)
-    dose, buf, counts = deposit(recv, rows, cols)
-    exposure, grad_high, grad_low = blur(dims, dose, target, zone, zone_weights)
-    slot_grad = sample(grad_high, grad_low, buf, counts)
-    return exposure, give_back(n, slot_grad, shot_tile)
+    count, tile = block_count.reshape(1, -1), shot_tile.reshape(1, -1)
+    recv, order = route(n, cols, shot_dose, shot_frac, shot_pos, count, tile)
+    dose, buf, spans = deposit(recv, rows, cols)
+    exposure, grad_high, grad_low = blur(dims, dose, target, zone, zone_weights.T)
+    slot_grad = sample(n, grad_high, grad_low, buf, spans)
+    return exposure, give_back(n, slot_grad, tile, order)
 
 
 def solution(mesh):

time: 104 us -> 84.7 us (0.81)
  Pallas kernels: 92.4 us -> 71.7 us
  local copies, waits for them, and re-layouts: 10.4 us -> 11.8 us
    pallas_call x1, Pallas kernels: 26.6 us -> 10.6 us  [give_back(): pl.pallas_call(functools.partial(return_kernel, n), out_shape=jax.ShapeDt...]
    pallas_call x1, Pallas kernels: 34.1 us -> 31.8 us  [blur(): pl.pallas_call(functools.partial(blur_kernel, dims), out_shape=[jax.Shape...]
    pallas_call x1, Pallas kernels: 14.5 us -> 13 us  [route(): pl.pallas_call(functools.partial(route_kernel, n, cols), out_shape=[jax.S...]
    unnamed x22 -> x28, local copies, waits for them, and re-layouts: 10.4 us -> 11.8 us
where the time goes in v1:
time: 84.7 us; the launch traced here: 84.2 us
  Pallas kernels  71.7 us (85%)
  local copies, waits for them, and re-layouts  11.8 us (14%)
    pallas_call x1, Pallas kernels, blur(): pl.pallas_call(functools.partial(blur_kernel, dims), out_shape=[jax.Shape...  31.8 us
    pallas_call x1, Pallas kernels, route(): pl.pallas_call(functools.partial(route_kernel, n, cols), out_shape=[jax.S...  13 us
    unnamed x28, local copies, waits for them, and re-layouts  11.8 us
    pallas_call x1, Pallas kernels, give_back(): pl.pallas_call(functools.partial(return_kernel, n), out_shape=jax.ShapeDt...  10.6 us
    pallas_call x1, Pallas kernels, deposit(): pl.pallas_call(deposit_kernel, out_shape=[jax.ShapeDtypeStruct((rows, col...  8.5 us
    pallas_call x1, Pallas kernels, sample(): pl.pallas_call(sample_kernel, out_shape=jax.ShapeDtypeStruct((n, 8, LANES...  7.77 us

profile of v1, /device:TPU:1, one launch (start us, length us, event | category | flops | bytes accessed | tf_op | source)
XLA Modules:
  0.0 84.2 jit_solution(11944726380333084645)
XLA Ops:
  0.6 0.0 copy-start.5
  0.6 0.7 copy-done.5
  1.4 0.0 copy-start.6
  1.4 0.7 copy-done.6
  2.1 0.0 copy-start.7
  2.1 0.7 copy-done.7
  2.8 0.0 copy-start.10
  2.8 0.7 copy-done.10
  3.5 0.0 copy-start.12
  3.5 0.7 copy-done.12
  4.1 13.0 %route.1 = (f32[32,8,128]{2,1,0:T(8,128)S(1)}, s32[32,128]{1,0:T(8,128)S(1)}) custom-call(f32[32,128]{1,0:T(8,128)S(1)} %copy-done.6, f32[2,32,128]{2,1,0:T(8,128)S(1)} %copy-done.5, s32[32,128]{1,0:T(8,128)S(1)} %copy-done.7, s32[1,32]{1,0:T(1,128)S(1)} %bitcast.6, s32[1,32]{1,0:T(1,128)S(1)} %bitcast.4), custom_call_target="tpu_custom_call" | custom-call | bytes 30000000 | tf_op jit(solution)/shard_map/route/pallas_call | solution.py:186
  17.2 8.5 %deposit.1 = (f32[256,1024]{1,0:T(8,128)S(1)}, f32[264,8,128]{2,1,0:T(8,128)S(1)}, s32[8,128]{1,0:T(8,128)S(1)}) custom-call(f32[32,8,128]{2,1,0:T(8,128)S(1)} %get-tuple-element.10.recv), custom_call_target="tpu_custom_call" | custom-call | bytes 24000000 | tf_op jit(solution)/shard_map/deposit/pallas_call | solution.py:351
  25.7 0.0 copy-start
  25.7 1.2 %copy-done = f32[256,1024]{1,0:T(8,128)S(1)} copy-done((f32[256,1024]{1,0:T(8,128)S(1)}, f32[256,1024]{1,0:T(8,128)}, u32[]{:S(2)}) %copy-start) | copy-done | bytes 1048600
  26.9 0.0 copy-start.1
  26.9 1.1 %copy-done.1 = bf16[3,512,256]{2,1,0:T(8,128)(2,1)S(1)} copy-done((bf16[3,512,256]{2,1,0:T(8,128)(2,1)S(1)}, bf16[3,512,256]{2,1,0:T(8,128)(2,1)}, u32[]{:S(2)}) %copy-start.1) | copy-done | bytes 786456
  28.1 0.0 copy-start.2
  28.1 1.1 %copy-done.2 = bf16[3,512,256]{2,1,0:T(8,128)(2,1)S(1)} copy-done((bf16[3,512,256]{2,1,0:T(8,128)(2,1)S(1)}, bf16[3,512,256]{2,1,0:T(8,128)(2,1)}, u32[]{:S(2)}) %copy-start.2) | copy-done | bytes 786456
  29.2 0.0 copy-start.3
  29.2 0.9 %copy-done.3 = bf16[384,256]{1,0:T(8,128)(2,1)S(1)} copy-done((bf16[384,256]{1,0:T(8,128)(2,1)S(1)}, bf16[384,256]{1,0:T(8,128)(2,1)}, u32[]{:S(2)}) %copy-start.3) | copy-done | bytes 196632
  30.1 0.0 copy-start.4
  30.1 0.9 %copy-done.4 = bf16[384,256]{1,0:T(8,128)(2,1)S(1)} copy-done((bf16[384,256]{1,0:T(8,128)(2,1)S(1)}, bf16[384,256]{1,0:T(8,128)(2,1)}, u32[]{:S(2)}) %copy-start.4) | copy-done | bytes 196632
  31.0 0.0 copy-start.8
  31.0 0.7 copy-done.8
  31.7 0.0 copy-start.9
  31.7 0.7 copy-done.9
  32.4 31.8 %blur.1 = (f32[256,1024]{1,0:T(8,128)S(1)}, bf16[256,1024]{1,0:T(8,128)(2,1)S(1)}, bf16[256,1024]{1,0:T(8,128)(2,1)S(1)}) custom-call(f32[256,1024]{1,0:T(8,128)S(1)} %get-tuple-element.11.dose, f32[256,1024]{1,0:T(8,128)S(1)} %copy-done, s32[4,16]{1,0:T(4,128)S(1)} %copy-done.8, f32[3,8]{1,0:T(4,128)S(1)} %bitcast.3, bf16[384,256]{1,0:T(8,128)(2,1)S(1)} %copy-done.4, ...), custom_call_target="tpu_custom_call" | custom-call | bytes 75000000 | tf_op jit(solution)/shard_map/blur/pallas_call | solution.py:710
  64.2 0.0 copy-start.11
  64.2 7.8 %sample.1.grads = f32[32,8,128]{2,1,0:T(8,128)S(1)} custom-call(bf16[256,1024]{1,0:T(8,128)(2,1)S(1)} %get-tuple-element.13.grad_high, bf16[256,1024]{1,0:T(8,128)(2,1)S(1)} %get-tuple-element.14.grad_low, f32[264,8,128]{2,1,0:T(8,128)S(1)} %get-tuple-element.15.buf, s32[8,128]{1,0:T(8,128)S(1)} %get-tuple-element.16.spans), custom_call_target="tpu_custom_call" | custom-call | bytes 24000000 | tf_op jit(solution)/shard_map/sample/pallas_call | solution.py:424
  72.0 0.0 copy-done.11
  72.0 10.6 %give_back.1 = f32[32,128]{1,0:T(8,128)S(1)} custom-call(f32[32,8,128]{2,1,0:T(8,128)S(1)} %sample.1.grads, s32[1,32]{1,0:T(1,128)S(1)} %bitcast.5, s32[32,128]{1,0:T(8,128)S(1)} %get-tuple-element.17.order), custom_call_target="tpu_custom_call" | custom-call | bytes 30000000 | tf_op jit(solution)/shard_map/give_back/pallas_call | solution.py:225
  82.6 1.0 %copy.16 = f32[256,1024]{1,0:T(8,128)} copy(f32[256,1024]{1,0:T(8,128)S(1)} %get-tuple-element.20) | data formatting | bytes 2097152
  83.6 0.6 copy.17
Async XLA Ops:
  0.6 0.8 copy-start.5
  1.4 0.7 copy-start.6
  2.1 0.7 copy-start.7
  2.8 0.7 copy-start.10
  3.5 0.7 copy-start.12
  25.7 1.2 %copy-start = (f32[256,1024]{1,0:T(8,128)S(1)}, f32[256,1024]{1,0:T(8,128)}, u32[]{:S(2)}) copy-start(f32[256,1024]{1,0:T(8,128)} %target_far.1) | copy-start | bytes 3145732
  26.9 1.1 %copy-start.1 = (bf16[3,512,256]{2,1,0:T(8,128)(2,1)S(1)}, bf16[3,512,256]{2,1,0:T(8,128)(2,1)}, u32[]{:S(2)}) copy-start(bf16[3,512,256]{2,1,0:T(8,128)(2,1)} %constant.11.clone.col_low_far) | copy-start | bytes 2359300
  28.1 1.1 %copy-start.2 = (bf16[3,512,256]{2,1,0:T(8,128)(2,1)S(1)}, bf16[3,512,256]{2,1,0:T(8,128)(2,1)}, u32[]{:S(2)}) copy-start(bf16[3,512,256]{2,1,0:T(8,128)(2,1)} %constant.10.clone.col_high_far) | copy-start | bytes 2359300
  29.2 0.9 %copy-start.3 = (bf16[384,256]{1,0:T(8,128)(2,1)S(1)}, bf16[384,256]{1,0:T(8,128)(2,1)}, u32[]{:S(2)}) copy-start(bf16[384,256]{1,0:T(8,128)(2,1)} %constant.9.clone.row_low_far) | copy-start | bytes 589828
  30.1 0.9 %copy-start.4 = (bf16[384,256]{1,0:T(8,128)(2,1)S(1)}, bf16[384,256]{1,0:T(8,128)(2,1)}, u32[]{:S(2)}) copy-start(bf16[384,256]{1,0:T(8,128)(2,1)} %constant.8.clone.row_high_far) | copy-start | bytes 589828
  31.0 0.7 copy-start.8
  31.7 0.7 copy-start.9
  64.2 7.8 %copy-start.11 = (s32[32,1]{0,1:T(1,128)S(1)}, s32[32,1]{0,1:T(1,128)}, u32[]{:S(2)}) copy-start(s32[32,1]{0,1:T(1,128)} %param.16) | copy-start | bytes 388

commit v2 on v1

--- a/solution.py
+++ b/solution.py
@@ -48,27 +48,15 @@
     return dot(onehot, first) + dot(onehot, second) + dot(onehot, third)
 
 
-def tap(offset, sigma):
+def taps(offset, sigma):
     reach = np.arange(-HALO, HALO + 1).astype(np.float64)
-    total = np.exp(-reach * reach / (2.0 * sigma * sigma)).sum()
-    inside = np.abs(offset) <= HALO
-    return np.where(inside, np.exp(-(offset.astype(np.float64) ** 2) / (2.0 * sigma * sigma)) / total, 0.0)
-
-
-def halves(x):
-    x = np.asarray(x, np.float32)
-    high = x.astype(BF16)
-    return high, (x - high.astype(np.float32)).astype(BF16)
-
-
-def row_bands():
-    i, y = np.arange(2 * HALO)[:, None], np.arange(4 * HALO)[None, :]
-    return halves(np.concatenate([tap(y - HALO - i, sigma) for sigma in SIGMAS]))
-
-
-def col_bands():
-    x, c = np.arange(2 * CHUNK)[:, None], np.arange(CHUNK)[None, :]
-    return halves(np.stack([tap(x - SIDE - c, sigma) for sigma in SIGMAS]))
+    total = float(np.exp(-reach * reach / (2.0 * sigma * sigma)).sum())
+    value = jnp.exp(offset * offset * (-1.0 / (2.0 * sigma * sigma))) * (1.0 / total)
+    return jnp.where(jnp.abs(offset) <= float(HALO), value, 0.0)
+
+
+def far(x):
+    return pltpu.with_memory_space_constraint(x, pltpu.HBM)
 
 
 def slots_of(tile, width):
@@ -203,7 +191,7 @@
         ),
         cost_estimate=cost(10),
         name="route",
-    )(dose, frac, pos, count, tile)
+    )(*(far(x) for x in (dose, frac, pos, count, tile)))
 
 
 def return_kernel(n, grads, tile, order, out, back, send_sem, recv_sem):
@@ -237,7 +225,7 @@
         ),
         cost_estimate=cost(10),
         name="give_back",
-    )(grads, tile, order)
+    )(grads, far(tile), order)
 
 
 def shot_rows(buf, first, end):
@@ -364,7 +352,9 @@
     )(recv)
 
 
-def sample_kernel(grad_high, grad_low, buf, spans, out, values):
+def sample_kernel(grad_high, grad_low, buf, spans, exposure, out, exposure_out, values, sem):
+    leave = pltpu.make_async_copy(exposure, exposure_out, sem)
+    leave.start()
     n = out.shape[0]
     rows, cols = grad_high.shape
     bins = cols // CHUNK
@@ -416,36 +406,43 @@
         return at
 
     lax.fori_loop(0, n, spread, [jnp.int32(s * LANES) for s in starts])
-
-
-def sample(n, grad_high, grad_low, buf, spans):
+    leave.wait()
+
+
+def sample(n, grad_high, grad_low, buf, spans, exposure):
     vmem = pl.BlockSpec(memory_space=pltpu.VMEM)
     smem = pl.BlockSpec(memory_space=pltpu.SMEM)
     return pl.pallas_call(
         sample_kernel,
-        out_shape=jax.ShapeDtypeStruct((n, 8, LANES), F32),
-        in_specs=[vmem, vmem, vmem, smem],
-        out_specs=vmem,
-        scratch_shapes=[pltpu.VMEM(buf.shape, F32)],
+        out_shape=[
+            jax.ShapeDtypeStruct((n, 8, LANES), F32),
+            jax.ShapeDtypeStruct(exposure.shape, F32),
+        ],
+        in_specs=[vmem, vmem, vmem, smem, pl.BlockSpec(memory_space=pl.ANY)],
+        out_specs=[vmem, pl.BlockSpec(memory_space=pl.ANY)],
+        scratch_shapes=[pltpu.VMEM(buf.shape, F32), pltpu.SemaphoreType.DMA],
         compiler_params=pltpu.CompilerParams(vmem_limit_bytes=16 * 2**20),
         cost_estimate=cost(8),
         name="sample",
-    )(grad_high, grad_low, buf, spans)
+    )(grad_high, grad_low, buf, spans, exposure)
 
 
 SIDES = ((-1, 0), (1, 0), (0, -1), (0, 1), (-1, -1), (-1, 1), (1, -1), (1, 1))
+PIECE_SIDE = (0, 0, 0, 0, 1, 1, 1, 1, 2, 3, 4, 5, 6, 7)
+OPPOSITE = (4, 5, 6, 7, 0, 1, 2, 3, 9, 8, 13, 12, 11, 10)
 
 
 def blur_kernel(
-    dims, dose, target_far, zone, zone_weights, row_high_far, row_low_far, col_high_far, col_low_far,
+    dims, dose, target_far, zone, zone_weights,
     exposure, grad_high, grad_low,
-    target, row_high, row_low, col_high, col_low, near_sem,
+    target, near_sem, mid_high, mid_low, edge_high, edge_low, col_high, col_low,
     zone_own, zone_in, halo_rows, halo_cols, halo_corners, dose_high, dose_low, part_high, part_low,
-    error, weight, dose_send, dose_recv, error_send, error_recv, zone_send, zone_recv,
+    mixed_high, mixed_low, error, weight, sends, recvs, zone_send, zone_recv,
 ):
     n_row, n_col = dims
     rows, cols = dose.shape
     wide = cols + 2 * SIDE
+    steps = cols // CHUNK
     row, col = lax.axis_index("row"), lax.axis_index("col")
 
     def exists(side):
@@ -461,58 +458,61 @@
         down, right = SIDES[side]
         return (row + down, col + right)
 
-    def opposite(side):
+    def landing(turn, piece):
+        if piece < 8:
+            return halo_rows.at[turn, piece // 4, :, pl.ds(piece % 4 * CHUNK, CHUNK)]
+        if piece < 10:
+            return halo_cols.at[turn, piece - 8]
+        return halo_corners.at[turn, piece - 10]
+
+    def edge(field, piece):
+        down, right = SIDES[PIECE_SIDE[piece]]
+        high = pl.ds(0, rows) if not down else (pl.ds(0, HALO) if down < 0 else pl.ds(rows - HALO, HALO))
+        if piece < 8:
+            across = pl.ds(piece % 4 * CHUNK, CHUNK)
+        else:
+            across = pl.ds(0, SIDE) if right < 0 else pl.ds(cols - SIDE, SIDE)
+        return field.at[high, across]
+
+    def halo_copy(field, turn, piece):
+        return pltpu.make_async_remote_copy(
+            src_ref=edge(field, piece),
+            dst_ref=landing(turn, OPPOSITE[piece]),
+            send_sem=sends.at[turn, piece],
+            recv_sem=recvs.at[turn, OPPOSITE[piece]],
+            device_id=neighbour(PIECE_SIDE[piece]),
+            device_id_type=MESH,
+        )
+
+    def zone_copy(side):
         down, right = SIDES[side]
-        return SIDES.index((-down, -right))
-
-    def landing(turn, side):
-        if side < 2:
-            return halo_rows.at[turn, side]
-        if side < 4:
-            return halo_cols.at[turn, side - 2]
-        return halo_corners.at[turn, side - 4]
-
-    def edge(field, side):
-        down, right = SIDES[side]
-        high = slice(None) if not down else (pl.ds(0, HALO) if down < 0 else pl.ds(rows - HALO, HALO))
-        across = slice(None) if not right else (pl.ds(0, SIDE) if right < 0 else pl.ds(cols - SIDE, SIDE))
-        return field.at[high, across]
-
-    def halo_copy(field, turn, side):
-        sends, recvs = (dose_send, dose_recv) if turn == 0 else (error_send, error_recv)
+        there = SIDES.index((-down, -right))
         return pltpu.make_async_remote_copy(
-            src_ref=edge(field, side),
-            dst_ref=landing(turn, opposite(side)),
-            send_sem=sends.at[side],
-            recv_sem=recvs.at[opposite(side)],
+            src_ref=zone_own,
+            dst_ref=zone_in.at[there],
+            send_sem=zone_send.at[side],
+            recv_sem=zone_recv.at[there],
             device_id=neighbour(side),
             device_id_type=MESH,
         )
 
-    def zone_copy(side):
-        return pltpu.make_async_remote_copy(
-            src_ref=zone_own,
-            dst_ref=zone_in.at[opposite(side)],
-            send_sem=zone_send.at[side],
-            recv_sem=zone_recv.at[opposite(side)],
-            device_id=neighbour(side),
-            device_id_type=MESH,
-        )
-
-    near = [
-        pltpu.make_async_copy(far, close, near_sem.at[i])
-        for i, (far, close) in enumerate(
-            (
-                (row_high_far, row_high),
-                (row_low_far, row_low),
-                (col_high_far, col_high),
-                (col_low_far, col_low),
-                (target_far, target),
-            )
-        )
-    ]
-    for copy in near:
-        copy.start()
+    def by_side(pieces, act):
+        for side in sorted({PIECE_SIDE[piece] for piece in pieces}, key=[PIECE_SIDE[p] for p in pieces].index):
+
+            @pl.when(exists(side))
+            def _(side=side):
+                for piece in pieces:
+                    if PIECE_SIDE[piece] == side:
+                        act(piece)
+
+    def send(field, turn, pieces):
+        by_side(pieces, lambda piece: halo_copy(field, turn, piece).start())
+
+    def await_halo(field, turn, pieces):
+        by_side(pieces, lambda piece: halo_copy(field, turn, OPPOSITE[piece]).wait_recv())
+
+    near = pltpu.make_async_copy(target_far, target, near_sem)
+    near.start()
     barrier = pltpu.get_barrier_semaphore()
     zone_own[...] = jnp.zeros_like(zone_own)
     zone_own[0 : zone.shape[0], 0 : zone.shape[1]] = zone[...]
@@ -521,8 +521,12 @@
         @pl.when(jnp.logical_not(exists(side)))
         def _(side=side):
             for turn in range(2):
-                spot = landing(turn, side)
-                spot[...] = jnp.zeros_like(spot)
+                if side < 2:
+                    halo_rows[turn, side] = jnp.zeros((HALO, cols), F32)
+                elif side < 4:
+                    halo_cols[turn, side - 2] = jnp.zeros((rows, SIDE), F32)
+                else:
+                    halo_corners[turn, side - 4] = jnp.zeros((HALO, SIDE), F32)
             zone_in[side] = jnp.zeros_like(zone_own)
 
     for side in range(8):
@@ -531,23 +535,29 @@
         def _(side=side):
             pl.semaphore_signal(barrier, inc=1, device_id=neighbour(side), device_id_type=MESH)
 
+    for kernel, sigma in enumerate(SIGMAS):
+        shape = (2 * HALO, 4 * HALO)
+        high, low = split(taps((iota(shape, 1) - iota(shape, 0) - HALO).astype(F32), sigma))
+        for band, mid, edges in ((high, mid_high, edge_high), (low, mid_low, edge_low)):
+            mid[kernel * 2 * HALO : (kernel + 1) * 2 * HALO] = band
+            for e in range(2):
+                edges[e, kernel * HALO : (kernel + 1) * HALO] = band[e * HALO : (e + 1) * HALO]
+        shape = (2 * CHUNK, CHUNK)
+        high, low = split(taps((iota(shape, 0) - iota(shape, 1) - SIDE).astype(F32), sigma))
+        col_high[kernel] = high
+        col_low[kernel] = low
+
     tall = 1 + jnp.where(row > 0, 1, 0) + jnp.where(row < n_row - 1, 1, 0)
     broad = 1 + jnp.where(col > 0, 1, 0) + jnp.where(col < n_col - 1, 1, 0)
     pl.semaphore_wait(barrier, tall * broad - 1)
-
     for side in range(8):
 
         @pl.when(exists(side))
         def _(side=side):
-            halo_copy(dose, 0, side).start()
             zone_copy(side).start()
 
-    def await_halo(field, turn, sides):
-        for side in sides:
-
-            @pl.when(exists(side))
-            def _(side=side):
-                halo_copy(field, turn, opposite(side)).wait_recv()
+    send(dose, 0, (8, 9, 0, 1, 4, 5, 11, 13))
+    send(dose, 0, (2, 3, 6, 7, 10, 12))
 
     def put_dose(value, first_row, first_col):
         high, low = split(value)
@@ -555,79 +565,90 @@
         dose_high[here] = high
         dose_low[here] = low
 
-    def along_cols(field, kernel):
-        count = field.shape[0]
-        stacked = [
-            jnp.concatenate([part[:, b : b + 2 * CHUNK] for b in range(0, cols, CHUNK)], axis=0)
-            for part in split(field)
-        ]
-        high, low = stacked
-        out = (
-            dot(high, col_high[kernel]) + dot(low, col_high[kernel]) + dot(high, col_low[kernel])
-        )
-        return jnp.concatenate(
-            [out[i * count : (i + 1) * count] for i in range(cols // CHUNK)], axis=1
-        )
-
-    windows = {
-        "top": (0, HALO, 0, 0),
-        "mid": (HALO, 2 * HALO, HALO, 0),
-        "low": (rows - HALO, HALO, 2 * HALO, HALO),
-    }
-
-    def row_blur(kernel, window, in_high, in_low):
-        first, count, begin, band = windows[window]
-        take = pl.ds(kernel * 2 * HALO + band, count)
-        here = pl.ds(begin, 4 * HALO)
-        high, low = row_high[take], row_low[take]
-        return dot(high, in_high[here]) + dot(low, in_high[here]) + dot(high, in_low[here])
-
-    def forward(window):
-        first, count, _, _ = windows[window]
-        total = [jnp.zeros((HALO, cols), F32) for _ in range(count // HALO)]
+    def put_part(value, square, first_col):
+        across = pl.ds(first_col, value.shape[1])
+        here = pl.ds(square * HALO, HALO)
         for kernel in range(3):
-            field = along_cols(row_blur(kernel, window, dose_high, dose_low), kernel)
-            for i in range(count // HALO):
-                square = 8 * kernel + 1 + first // HALO + i
-                factor = weight[square : square + 1, SIDE : SIDE + cols]
-                total[i] = total[i] + factor * field[i * HALO : (i + 1) * HALO]
-        for i in range(count // HALO):
-            here = pl.ds(first + i * HALO, HALO)
-            exposure[here] = total[i]
-            error[here] = total[i] - target[here]
-
-    def put_part(value, first_row, first_col):
-        across = pl.ds(first_col, value.shape[1])
-        for i in range(value.shape[0] // HALO):
-            square = first_row // HALO + i
-            here = pl.ds(first_row + i * HALO, HALO)
-            piece = value[i * HALO : (i + 1) * HALO]
+            factor = weight[8 * kernel + square : 8 * kernel + square + 1, across]
+            high, low = split(factor * value)
+            part_high[kernel, here, across] = high
+            part_low[kernel, here, across] = low
+
+    def tile_forward(edges, j):
+        tile = pl.ds(j * CHUNK, CHUNK)
+
+        def keep(band_high, band_low, first_row, first_out, count):
+            here = pl.ds(first_row, 4 * HALO)
+            in_high, in_low = dose_high[here, tile], dose_low[here, tile]
+            field = dot(band_high, in_high) + dot(band_low, in_high) + dot(band_high, in_low)
+            high, low = split(field)
             for kernel in range(3):
-                factor = weight[8 * kernel + square : 8 * kernel + square + 1, across]
-                high, low = split(factor * piece)
-                part_high[kernel, here, across] = high
-                part_low[kernel, here, across] = low
-
-    def backward(window):
-        first, count, _, _ = windows[window]
-        total = jnp.zeros((count, cols), F32)
+                part = slice(kernel * count, (kernel + 1) * count)
+                mixed_high[edges, kernel, first_out : first_out + count, tile] = high[part]
+                mixed_low[edges, kernel, first_out : first_out + count, tile] = low[part]
+
+        if edges:
+            keep(edge_high[0], edge_low[0], 0, 0, HALO)
+            keep(edge_high[1], edge_low[1], 2 * HALO, HALO, HALO)
+        else:
+            keep(mid_high[...], mid_low[...], HALO, 0, 2 * HALO)
+
+    def along_cols(edges, u, kernel):
+        take = pl.ds(u * CHUNK, 2 * CHUNK)
+        high, low = mixed_high[edges, kernel, :, take], mixed_low[edges, kernel, :, take]
+        return dot(high, col_high[kernel]) + dot(low, col_high[kernel]) + dot(high, col_low[kernel])
+
+    def window_forward(edges, u):
+        squares = (1, rows // HALO) if edges else (2, 3)
+        total = [jnp.zeros((HALO, CHUNK), F32) for _ in range(2)]
         for kernel in range(3):
-            field = row_blur(kernel, window, part_high.at[kernel], part_low.at[kernel])
-            total = total + along_cols(field, kernel)
-        high, low = split(total)
-        here = pl.ds(first, count)
-        grad_high[here] = high
-        grad_low[here] = low
+            field = along_cols(edges, u, kernel)
+            for half, square in enumerate(squares):
+                line = 8 * kernel + square
+                factor = weight[line : line + 1, SIDE + u * CHUNK : SIDE + (u + 1) * CHUNK]
+                total[half] = total[half] + factor * field[half * HALO : (half + 1) * HALO]
+        for half, square in enumerate(squares):
+            here = pl.ds((square - 1) * HALO, HALO), pl.ds(u * CHUNK, CHUNK)
+            exposure[here] = total[half]
+            wrong = total[half] - target[here]
+            error[here] = wrong
+            put_part(wrong, square, SIDE + u * CHUNK)
+
+    def tile_backward(edges, j):
+        tile = pl.ds(j * CHUNK, CHUNK)
+
+        def keep(kernel, band_high, band_low, first_row, first_out, count):
+            here = pl.ds(first_row, 4 * HALO)
+            in_high, in_low = part_high[kernel, here, tile], part_low[kernel, here, tile]
+            field = dot(band_high, in_high) + dot(band_low, in_high) + dot(band_high, in_low)
+            high, low = split(field)
+            mixed_high[edges, kernel, first_out : first_out + count, tile] = high
+            mixed_low[edges, kernel, first_out : first_out + count, tile] = low
+
+        for kernel in range(3):
+            if edges:
+                part = pl.ds(kernel * HALO, HALO)
+                keep(kernel, edge_high[0, part], edge_low[0, part], 0, 0, HALO)
+                keep(kernel, edge_high[1, part], edge_low[1, part], 2 * HALO, HALO, HALO)
+            else:
+                part = pl.ds(kernel * 2 * HALO, 2 * HALO)
+                keep(kernel, mid_high[part], mid_low[part], HALO, 0, 2 * HALO)
+
+    def window_backward(edges, u):
+        squares = (1, rows // HALO) if edges else (2, 3)
+        high, low = split(sum(along_cols(edges, u, kernel) for kernel in range(3)))
+        for half, square in enumerate(squares):
+            here = pl.ds((square - 1) * HALO, HALO), pl.ds(u * CHUNK, CHUNK)
+            grad_high[here] = high[half * HALO : (half + 1) * HALO]
+            grad_low[here] = low[half * HALO : (half + 1) * HALO]
 
     def zone_table():
         sub, lane = iota((8, LANES), 0), iota((8, LANES), 1)
         high, across = zone.shape
-        own = pltpu.roll(pltpu.roll(zone_own[...], 1, axis=0), 2, axis=1)
-        table = own
+        table = pltpu.roll(pltpu.roll(zone_own[...], 1, axis=0), 2, axis=1)
         for side in range(8):
             down, right = SIDES[side]
-            got = zone_in[side]
-            got = pltpu.roll(got, (1 + down * high) % 8, axis=0)
+            got = pltpu.roll(zone_in[side], (1 + down * high) % 8, axis=0)
             got = pltpu.roll(got, (2 + right * across) % LANES, axis=1)
             row_ok = (sub == 0) if down < 0 else (sub == high + 1) if down > 0 else (sub >= 1) & (sub <= high)
             col_ok = (
@@ -640,62 +661,76 @@
             for z in range(ZONES):
                 value = jnp.where(table == z, zone_weights[kernel, z], value)
             picked.append(value)
-        spread = iota((LANES, wide), 0) == iota((LANES, wide), 1) // HALO
-        return picked, spread
+        return jnp.concatenate(picked, axis=0)
 
     put_dose(dose[...], HALO, SIDE)
     for side in range(8):
 
         @pl.when(exists(side))
         def _(side=side):
-            zone_copy(opposite(side)).wait_recv()
-
-    picked, spread = zone_table()
-    spread = jnp.where(spread, 1.0, 0.0).astype(BF16)
-    stacked = jnp.concatenate(picked, axis=0)
-    first_part = stacked.astype(BF16)
-    rest = stacked - first_part.astype(F32)
-    second_part = rest.astype(BF16)
-    third_part = (rest - second_part.astype(F32)).astype(BF16)
-    weight[...] = dot(first_part, spread) + dot(second_part, spread) + dot(third_part, spread)
-
-    for copy in near:
-        copy.wait()
-    await_halo(dose, 0, (2, 3))
+            down, right = SIDES[side]
+            zone_copy(SIDES.index((-down, -right))).wait_recv()
+
+    spread = jnp.where(iota((LANES, wide), 0) == iota((LANES, wide), 1) // HALO, 1.0, 0.0).astype(BF16)
+    table = zone_table()
+    for _ in range(3):
+        piece = table.astype(BF16)
+        weight[...] = dot(piece, spread) if _ == 0 else weight[...] + dot(piece, spread)
+        table = table - piece.astype(F32)
+
+    def sweep(tile, window, edges, before, after):
+        for u in range(steps):
+            before(u)
+            if u == 0:
+                tile(edges, 0)
+            tile(edges, u + 1)
+            window(edges, u)
+            after(u)
+
+    def nothing(u):
+        return None
+
+    near.wait()
+    await_halo(dose, 0, (8, 9))
     put_dose(halo_cols[0, 0], HALO, 0)
     put_dose(halo_cols[0, 1], HALO, SIDE + cols)
-    forward("mid")
-    await_halo(dose, 0, (0, 1, 4, 5, 6, 7))
-    for place, first_row in ((0, 0), (1, HALO + rows)):
-        put_dose(halo_rows[0, place], first_row, SIDE)
-        put_dose(halo_corners[0, 2 * place], first_row, 0)
-        put_dose(halo_corners[0, 2 * place + 1], first_row, SIDE + cols)
-    forward("top")
-    forward("low")
+    sweep(tile_forward, window_forward, 0, nothing, nothing)
+
+    def arrive(turn, field, put, u):
+        chunks = (0, 1) if u == 0 else (u + 1,) if u + 1 < steps else ()
+        corners = (10, 12) if u == 0 else (11, 13) if u == steps - 1 else ()
+        await_halo(field, turn, (*chunks, *(4 + c for c in chunks), *corners))
+        for side, square in ((0, 0), (1, rows // HALO + 1)):
+            for c in chunks:
+                put(halo_rows[turn, side, :, c * CHUNK : (c + 1) * CHUNK], square, SIDE + c * CHUNK)
+            if u == 0:
+                put(halo_corners[turn, 2 * side], square, 0)
+            if u == steps - 1:
+                put(halo_corners[turn, 2 * side + 1], square, SIDE + cols)
+
+    def send_error(u):
+        sides = (8, 10, 12) if u == 0 else (9, 11, 13) if u == steps - 1 else ()
+        send(error, 1, (u, 4 + u, *sides))
+
+    sweep(
+        tile_forward,
+        window_forward,
+        1,
+        lambda u: arrive(0, dose, lambda value, square, at: put_dose(value, square * HALO, at), u),
+        send_error,
+    )
+    await_halo(error, 1, (8, 9))
+    for side, at in ((0, 0), (1, SIDE + cols)):
+        for square in range(rows // HALO):
+            put_part(halo_cols[1, side, square * HALO : (square + 1) * HALO], 1 + square, at)
+    sweep(tile_backward, window_backward, 0, nothing, nothing)
+    sweep(tile_backward, window_backward, 1, lambda u: arrive(1, error, put_part, u), nothing)
+    by_side(range(14), lambda piece: halo_copy(dose, 0, piece).wait_send())
+    by_side(range(14), lambda piece: halo_copy(error, 1, piece).wait_send())
     for side in range(8):
 
         @pl.when(exists(side))
         def _(side=side):
-            halo_copy(error, 1, side).start()
-
-    put_part(error[...], HALO, SIDE)
-    await_halo(error, 1, (2, 3))
-    put_part(halo_cols[1, 0], HALO, 0)
-    put_part(halo_cols[1, 1], HALO, SIDE + cols)
-    backward("mid")
-    await_halo(error, 1, (0, 1, 4, 5, 6, 7))
-    for place, first_row in ((0, 0), (1, HALO + rows)):
-        put_part(halo_rows[1, place], first_row, SIDE)
-        put_part(halo_corners[1, 2 * place], first_row, 0)
-        put_part(halo_corners[1, 2 * place + 1], first_row, SIDE + cols)
-    backward("top")
-    backward("low")
-    for side in range(8):
-
-        @pl.when(exists(side))
-        def _(side=side):
-            halo_copy(dose, 0, side).wait_send()
-            halo_copy(error, 1, side).wait_send()
             zone_copy(side).wait_send()
 
 
@@ -704,9 +739,7 @@
     wide, high = cols + 2 * SIDE, rows + 2 * HALO
     vmem = pl.BlockSpec(memory_space=pltpu.VMEM)
     smem = pl.BlockSpec(memory_space=pltpu.SMEM)
-    far = pl.BlockSpec(memory_space=pltpu.HBM)
-    dma = pltpu.SemaphoreType.DMA((8,))
-    bands = (*row_bands(), *col_bands())
+    dma = pltpu.SemaphoreType.DMA
     return pl.pallas_call(
         functools.partial(blur_kernel, dims),
         out_shape=[
@@ -714,12 +747,17 @@
             jax.ShapeDtypeStruct((rows, cols), BF16),
             jax.ShapeDtypeStruct((rows, cols), BF16),
         ],
-        in_specs=[vmem, far, vmem, smem, far, far, far, far],
+        in_specs=[vmem, pl.BlockSpec(memory_space=pl.ANY), vmem, smem],
         out_specs=[vmem] * 3,
         scratch_shapes=[
             pltpu.VMEM((rows, cols), F32),
-            *[pltpu.VMEM(band.shape, BF16) for band in bands],
-            pltpu.SemaphoreType.DMA((5,)),
+            dma,
+            pltpu.VMEM((6 * HALO, 4 * HALO), BF16),
+            pltpu.VMEM((6 * HALO, 4 * HALO), BF16),
+            pltpu.VMEM((2, 3 * HALO, 4 * HALO), BF16),
+            pltpu.VMEM((2, 3 * HALO, 4 * HALO), BF16),
+            pltpu.VMEM((3, 2 * CHUNK, CHUNK), BF16),
+            pltpu.VMEM((3, 2 * CHUNK, CHUNK), BF16),
             pltpu.VMEM((8, LANES), I32),
             pltpu.VMEM((8, 8, LANES), I32),
             pltpu.VMEM((2, 2, HALO, cols), F32),
@@ -729,16 +767,18 @@
             pltpu.VMEM((high, wide), BF16),
             pltpu.VMEM((3, high, wide), BF16),
             pltpu.VMEM((3, high, wide), BF16),
+            pltpu.VMEM((2, 3, 2 * HALO, wide), BF16),
+            pltpu.VMEM((2, 3, 2 * HALO, wide), BF16),
             pltpu.VMEM((rows, cols), F32),
             pltpu.VMEM((24, wide), F32),
-            dma, dma, dma, dma, dma, dma,
+            dma((2, 14)), dma((2, 14)), dma((8,)), dma((8,)),
         ],
         compiler_params=pltpu.CompilerParams(
-            collective_id=1, has_side_effects=True, vmem_limit_bytes=32 * 2**20
+            collective_id=1, has_side_effects=True, vmem_limit_bytes=40 * 2**20
         ),
         cost_estimate=cost(25),
         name="blur",
-    )(dose, target, zone, zone_weights, *bands)
+    )(dose, far(target), far(zone), far(zone_weights))
 
 
 def per_device(dims, shot_dose, shot_frac, shot_pos, block_count, shot_tile, zone, zone_weights, target):
@@ -748,7 +788,7 @@
     recv, order = route(n, cols, shot_dose, shot_frac, shot_pos, count, tile)
     dose, buf, spans = deposit(recv, rows, cols)
     exposure, grad_high, grad_low = blur(dims, dose, target, zone, zone_weights.T)
-    slot_grad = sample(n, grad_high, grad_low, buf, spans)
+    slot_grad, exposure = sample(n, grad_high, grad_low, buf, spans, exposure)
     return exposure, give_back(n, slot_grad, tile, order)
 
 

time: 84.7 us -> 66.3 us (0.78)
  local copies, waits for them, and re-layouts: 11.8 us -> 0.61 us
  Pallas kernels: 71.7 us -> 64.8 us
    unnamed x28 -> x1, local copies, waits for them, and re-layouts: 11.8 us -> 0.61 us
    pallas_call x1, Pallas kernels: 31.8 us -> 24.5 us  [blur(): pl.pallas_call(functools.partial(blur_kernel, dims), out_shape=[jax.Shape...]
    pallas_call x1, Pallas kernels: 10.6 us -> 14.3 us  [give_back(): pl.pallas_call(functools.partial(return_kernel, n), out_shape=jax.ShapeDt...]
    pallas_call x1, Pallas kernels: 7.77 us -> 5.64 us  [sample(): pl.pallas_call(sample_kernel, out_shape=[jax.ShapeDtypeStruct((n, 8, LANE...]
    pallas_call x1, Pallas kernels: 8.5 us -> 6.51 us  [deposit(): pl.pallas_call(deposit_kernel, out_shape=[jax.ShapeDtypeStruct((rows, col...]
where the time goes in v2:
time: 66.3 us; the launch traced here: 66.1 us
  Pallas kernels  64.8 us (98%)
  between operations  0.67 us (1%)
    pallas_call x1, Pallas kernels, blur(): pl.pallas_call(functools.partial(blur_kernel, dims), out_shape=[jax.Shape...  24.5 us
    pallas_call x1, Pallas kernels, give_back(): pl.pallas_call(functools.partial(return_kernel, n), out_shape=jax.ShapeDt...  14.3 us
    pallas_call x1, Pallas kernels, route(): pl.pallas_call(functools.partial(route_kernel, n, cols), out_shape=[jax.S...  13.9 us
    pallas_call x1, Pallas kernels, deposit(): pl.pallas_call(deposit_kernel, out_shape=[jax.ShapeDtypeStruct((rows, col...  6.51 us
    pallas_call x1, Pallas kernels, sample(): pl.pallas_call(sample_kernel, out_shape=[jax.ShapeDtypeStruct((n, 8, LANE...  5.64 us

profile of v2, /device:TPU:1, one launch (start us, length us, event | category | flops | bytes accessed | tf_op | source)
XLA Modules:
  0.0 66.1 jit_solution(9064718531719172395)
XLA Ops:
  0.6 13.9 %route.1 = (f32[32,8,128]{2,1,0:T(8,128)S(1)}, s32[32,128]{1,0:T(8,128)S(1)}) custom-call(f32[32,128]{1,0:T(8,128)} %dose.1, f32[2,32,128]{2,1,0:T(8,128)} %frac.1, s32[32,128]{1,0:T(8,128)} %pos.1, s32[1,32]{1,0:T(1,128)} %bitcast.6, s32[1,32]{1,0:T(1,128)} %bitcast.3), custom_call_target="tpu_custom_call" | custom-call | bytes 30000000 | tf_op jit(solution)/shard_map/route/pallas_call | solution.py:174
  14.5 6.5 %deposit.1 = (f32[256,1024]{1,0:T(8,128)S(1)}, f32[264,8,128]{2,1,0:T(8,128)S(1)}, s32[8,128]{1,0:T(8,128)S(1)}) custom-call(f32[32,8,128]{2,1,0:T(8,128)S(1)} %get-tuple-element.12.recv), custom_call_target="tpu_custom_call" | custom-call | bytes 24000000 | tf_op jit(solution)/shard_map/deposit/pallas_call | solution.py:339
  21.0 24.5 %blur.1 = (f32[256,1024]{1,0:T(8,128)S(1)}, bf16[256,1024]{1,0:T(8,128)(2,1)S(1)}, bf16[256,1024]{1,0:T(8,128)(2,1)S(1)}) custom-call(f32[256,1024]{1,0:T(8,128)S(1)} %get-tuple-element.13.dose, f32[256,1024]{1,0:T(8,128)} %target_far.1, s32[4,16]{1,0:T(4,128)} %zone.1, f32[3,8]{1,0:T(4,128)} %bitcast.5), custom_call_target="tpu_custom_call" | custom-call | bytes 75000000 | tf_op jit(solution)/shard_map/blur/pallas_call | solution.py:743
  45.5 5.6 %sample.1 = (f32[32,8,128]{2,1,0:T(8,128)S(1)}, f32[256,1024]{1,0:T(8,128)}) custom-call(bf16[256,1024]{1,0:T(8,128)(2,1)S(1)} %get-tuple-element.14.grad_high, bf16[256,1024]{1,0:T(8,128)(2,1)S(1)} %get-tuple-element.15.grad_low, f32[264,8,128]{2,1,0:T(8,128)S(1)} %get-tuple-element.16.buf, s32[8,128]{1,0:T(8,128)S(1)} %get-tuple-element.17.spans, ...), custom_call_target="tpu_custom_call" | custom-call | bytes 24000000 | tf_op jit(solution)/shard_map/sample/pallas_call | solution.py:415
  51.2 14.3 %give_back.1 = f32[32,128]{1,0:T(8,128)S(1)} custom-call(f32[32,8,128]{2,1,0:T(8,128)S(1)} %get-tuple-element.20.grads, s32[1,32]{1,0:T(1,128)} %bitcast.4, s32[32,128]{1,0:T(8,128)S(1)} %get-tuple-element.21.order), custom_call_target="tpu_custom_call" | custom-call | bytes 30000000 | tf_op jit(solution)/shard_map/give_back/pallas_call | solution.py:213
  65.4 0.6 copy.11

commit v3 on v2

--- a/solution.py
+++ b/solution.py
@@ -13,6 +13,7 @@
 ZONES = 8
 LANES = 128
 CHUNK = 256
+SHOTS = 512
 SIDE = 128
 SIGMAS = (0.125 * HALO, 0.25 * HALO, 0.5 * HALO)
 MESH = pl.DeviceIdType.MESH
@@ -230,8 +231,8 @@
 
 def shot_rows(buf, first, end):
     lane = iota((8, LANES), 1)
-    both = [jnp.where(lane < end, buf[first], 0.0), jnp.where(lane < end - LANES, buf[first + 1], 0.0)]
-    line = lambda f: jnp.concatenate([part[f : f + 1] for part in both], axis=1)
+    tiles = [jnp.where(lane < end - i * LANES, buf[first + i], 0.0) for i in range(SHOTS // LANES)]
+    line = lambda f: jnp.concatenate([tile[f : f + 1] for tile in tiles], axis=1)
     return line(0), line(1), line(2), line(3).astype(I32) - 1
 
 
@@ -293,29 +294,30 @@
         full = jnp.full((8, LANES), lane_at + amount, I32) >= LANES
         return at + amount, jnp.where(full, moved, merged)
 
-    def gather(i, carry):
-        block = recv[i]
-        for half in range(2):
-            index = half * n + i
-            carry = [
-                append(block, spans[q, index], spans[bins + q, index], carry[q]) for q in range(bins)
-            ]
-            block = pltpu.roll(block, 4, axis=0)
+    def gather(step, carry):
+        for i in range(4):
+            block = recv[4 * step + i]
+            for half in range(2):
+                index = half * n + 4 * step + i
+                carry = [
+                    append(block, spans[q, index], spans[bins + q, index], carry[q]) for q in range(bins)
+                ]
+                block = pltpu.roll(block, 4, axis=0)
         return carry
 
     starts = [q * tiles_of_bin(n) for q in range(bins)]
     empty = jnp.zeros((8, LANES), F32)
-    found = lax.fori_loop(0, n, gather, [(jnp.int32(s * LANES), empty) for s in starts])
+    found = lax.fori_loop(0, n // 4, gather, [(jnp.int32(s * LANES), empty) for s in starts])
     most = jnp.int32(0)
     for q, (at, last) in enumerate(found):
         buf[at >> 7] = jnp.where(lane < (at & (LANES - 1)), last, 0.0)
         buf[(at >> 7) + 1] = empty
-        most = jnp.maximum(most, (at - starts[q] * LANES + CHUNK - 1) >> 8)
+        most = jnp.maximum(most, (at - starts[q] * LANES + SHOTS - 1) >> SHOTS.bit_length() - 1)
     spans[0, LANES - 1] = most
 
     def deposit(chunk, carry):
         for q in range(bins):
-            first = starts[q] + 2 * chunk
+            first = starts[q] + SHOTS // LANES * chunk
             end = found[q][0] - first * LANES
             amount, frac_row, frac_col, place = shot_rows(buf, first, end)
             pixel_row = jnp.minimum(place >> shift, rows - 2)
@@ -363,8 +365,8 @@
 
     def sample(chunk, carry):
         for q in range(bins):
-            first = starts[q] + 2 * chunk
-            _, frac_row, frac_col, place = shot_rows(buf, first, CHUNK)
+            first = starts[q] + SHOTS // LANES * chunk
+            _, frac_row, frac_col, place = shot_rows(buf, first, SHOTS)
             pixel_row = jnp.minimum(place >> shift, rows - 2)
             high, low = col_table(place, frac_col, cols, q)
             window = slice(q * CHUNK, (q + 1) * CHUNK)
@@ -373,13 +375,13 @@
                 + dot(grad_low[:, window], high)
                 + dot(grad_high[:, window], low)
             )
-            here = iota((rows, CHUNK), 0)
+            here = iota((rows, SHOTS), 0)
             weight = jnp.where(
                 here == pixel_row, 1.0 - frac_row, jnp.where(here == pixel_row + 1, frac_row, 0.0)
             )
             got = jnp.sum(weight * along, axis=0, keepdims=True)
-            values[first, 0:1] = got[:, :LANES]
-            values[first + 1, 0:1] = got[:, LANES:]
+            for i in range(SHOTS // LANES):
+                values[first + i, 0:1] = got[:, i * LANES : (i + 1) * LANES]
         return carry
 
     lax.fori_loop(0, spans[0, LANES - 1], sample, 0)
@@ -392,7 +394,12 @@
         moved = pltpu.roll(both, (begin - at) & (LANES - 1), axis=1)
         return jnp.where((lane >= begin) & (lane < begin + amount), moved, 0.0)
 
-    def spread(i, at):
+    def spread(step, at):
+        for i in range(8):
+            at = spread_one(8 * step + i, at)
+        return at
+
+    def spread_one(i, at):
         at = list(at)
         both = []
         for half in range(2):
@@ -405,7 +412,7 @@
         out[i] = jnp.where(row == 0, both[0], jnp.where(row == 1, both[1], 0.0))
         return at
 
-    lax.fori_loop(0, n, spread, [jnp.int32(s * LANES) for s in starts])
+    lax.fori_loop(0, n // 8, spread, [jnp.int32(s * LANES) for s in starts])
     leave.wait()
 
 
@@ -596,7 +603,8 @@
     def along_cols(edges, u, kernel):
         take = pl.ds(u * CHUNK, 2 * CHUNK)
         high, low = mixed_high[edges, kernel, :, take], mixed_low[edges, kernel, :, take]
-        return dot(high, col_high[kernel]) + dot(low, col_high[kernel]) + dot(high, col_low[kernel])
+        both = dot(jnp.concatenate([high, low], axis=0), col_high[kernel])
+        return both[: 2 * HALO] + both[2 * HALO :] + dot(high, col_low[kernel])
 
     def window_forward(edges, u):
         squares = (1, rows // HALO) if edges else (2, 3)
@@ -679,11 +687,13 @@
         table = table - piece.astype(F32)
 
     def sweep(tile, window, edges, before, after):
+        ahead = 2
+        done = 0
         for u in range(steps):
             before(u)
-            if u == 0:
-                tile(edges, 0)
-            tile(edges, u + 1)
+            while done <= min(u + ahead, steps):
+                tile(edges, done)
+                done += 1
             window(edges, u)
             after(u)
 
@@ -697,15 +707,15 @@
     sweep(tile_forward, window_forward, 0, nothing, nothing)
 
     def arrive(turn, field, put, u):
-        chunks = (0, 1) if u == 0 else (u + 1,) if u + 1 < steps else ()
-        corners = (10, 12) if u == 0 else (11, 13) if u == steps - 1 else ()
+        chunks = (0, 1, 2) if u == 0 else (u + 2,) if u + 2 < steps else ()
+        corners = (10, 12) if u == 0 else (11, 13) if u == steps - 2 else ()
         await_halo(field, turn, (*chunks, *(4 + c for c in chunks), *corners))
         for side, square in ((0, 0), (1, rows // HALO + 1)):
             for c in chunks:
                 put(halo_rows[turn, side, :, c * CHUNK : (c + 1) * CHUNK], square, SIDE + c * CHUNK)
             if u == 0:
                 put(halo_corners[turn, 2 * side], square, 0)
-            if u == steps - 1:
+            if u == steps - 2:
                 put(halo_corners[turn, 2 * side + 1], square, SIDE + cols)
 
     def send_error(u):

time: 66.3 us -> 63.2 us (0.953)
  Pallas kernels: 64.8 us -> 61.7 us
    pallas_call x1, Pallas kernels: 5.64 us -> 4.39 us  [sample(): pl.pallas_call(sample_kernel, out_shape=[jax.ShapeDtypeStruct((n, 8, LANE...]
    pallas_call x1, Pallas kernels: 6.51 us -> 5.34 us  [deposit(): pl.pallas_call(deposit_kernel, out_shape=[jax.ShapeDtypeStruct((rows, col...]
where the time goes in v3:
time: 63.2 us; the launch traced here: 63 us
  Pallas kernels  61.7 us (98%)
  between operations  0.67 us (1%)
    pallas_call x1, Pallas kernels, blur(): pl.pallas_call(functools.partial(blur_kernel, dims), out_shape=[jax.Shape...  24.4 us
    pallas_call x1, Pallas kernels, route(): pl.pallas_call(functools.partial(route_kernel, n, cols), out_shape=[jax.S...  13.9 us
    pallas_call x1, Pallas kernels, give_back(): pl.pallas_call(functools.partial(return_kernel, n), out_shape=jax.ShapeDt...  13.7 us
    pallas_call x1, Pallas kernels, deposit(): pl.pallas_call(deposit_kernel, out_shape=[jax.ShapeDtypeStruct((rows, col...  5.34 us
    pallas_call x1, Pallas kernels, sample(): pl.pallas_call(sample_kernel, out_shape=[jax.ShapeDtypeStruct((n, 8, LANE...  4.39 us

profile of v3, /device:TPU:1, one launch (start us, length us, event | category | flops | bytes accessed | tf_op | source)
XLA Modules:
  0.0 63.0 jit_solution(5356321509987966186)
XLA Ops:
  0.6 13.9 %route.1 = (f32[32,8,128]{2,1,0:T(8,128)S(1)}, s32[32,128]{1,0:T(8,128)S(1)}) custom-call(f32[32,128]{1,0:T(8,128)} %dose.1, f32[2,32,128]{2,1,0:T(8,128)} %frac.1, s32[32,128]{1,0:T(8,128)} %pos.1, s32[1,32]{1,0:T(1,128)} %bitcast.6, s32[1,32]{1,0:T(1,128)} %bitcast.3), custom_call_target="tpu_custom_call" | custom-call | bytes 30000000 | tf_op jit(solution)/shard_map/route/pallas_call | solution.py:175
  14.5 5.3 %deposit.1 = (f32[256,1024]{1,0:T(8,128)S(1)}, f32[264,8,128]{2,1,0:T(8,128)S(1)}, s32[8,128]{1,0:T(8,128)S(1)}) custom-call(f32[32,8,128]{2,1,0:T(8,128)S(1)} %get-tuple-element.12.recv), custom_call_target="tpu_custom_call" | custom-call | bytes 24000000 | tf_op jit(solution)/shard_map/deposit/pallas_call | solution.py:341
  19.9 24.4 %blur.1 = (f32[256,1024]{1,0:T(8,128)S(1)}, bf16[256,1024]{1,0:T(8,128)(2,1)S(1)}, bf16[256,1024]{1,0:T(8,128)(2,1)S(1)}) custom-call(f32[256,1024]{1,0:T(8,128)S(1)} %get-tuple-element.13.dose, f32[256,1024]{1,0:T(8,128)} %target_far.1, s32[4,16]{1,0:T(4,128)} %zone.1, f32[3,8]{1,0:T(4,128)} %bitcast.5), custom_call_target="tpu_custom_call" | custom-call | bytes 75000000 | tf_op jit(solution)/shard_map/blur/pallas_call | solution.py:753
  44.3 4.4 %sample.1 = (f32[32,8,128]{2,1,0:T(8,128)S(1)}, f32[256,1024]{1,0:T(8,128)}) custom-call(bf16[256,1024]{1,0:T(8,128)(2,1)S(1)} %get-tuple-element.14.grad_high, bf16[256,1024]{1,0:T(8,128)(2,1)S(1)} %get-tuple-element.15.grad_low, f32[264,8,128]{2,1,0:T(8,128)S(1)} %get-tuple-element.16.buf, s32[8,128]{1,0:T(8,128)S(1)} %get-tuple-element.17.spans, ...), custom_call_target="tpu_custom_call" | custom-call | bytes 24000000 | tf_op jit(solution)/shard_map/sample/pallas_call | solution.py:422
  48.7 13.7 %give_back.1 = f32[32,128]{1,0:T(8,128)S(1)} custom-call(f32[32,8,128]{2,1,0:T(8,128)S(1)} %get-tuple-element.20.grads, s32[1,32]{1,0:T(1,128)} %bitcast.4, s32[32,128]{1,0:T(8,128)S(1)} %get-tuple-element.21.order), custom_call_target="tpu_custom_call" | custom-call | bytes 30000000 | tf_op jit(solution)/shard_map/give_back/pallas_call | solution.py:214
  62.4 0.6 copy.11

commit v4 on v3

--- a/solution.py
+++ b/solution.py
@@ -86,7 +86,7 @@
     barrier = pltpu.get_barrier_semaphore()
 
     def greet(step, carry):
-        peer = lax.rem(me + step, n)
+        peer = (me + step) & (n - 1)
         pl.semaphore_signal(barrier, inc=1, device_id=(row, peer), device_id_type=MESH)
         return carry
 
@@ -94,39 +94,55 @@
     return barrier
 
 
-def exchange(n, me, row, source, target, send_sem, recv_sem):
-    def copy_to(peer, slot):
+def exchange(n, me, row, source, target, send_sem, recv_sem, meanwhile):
+    def copy(peer, source_slots, target_slots):
         return pltpu.make_async_remote_copy(
-            src_ref=source.at[peer],
-            dst_ref=target.at[slot],
-            send_sem=send_sem.at[peer],
-            recv_sem=recv_sem.at[slot],
+            src_ref=source.at[source_slots],
+            dst_ref=target.at[target_slots],
+            send_sem=send_sem,
+            recv_sem=recv_sem,
             device_id=(row, peer),
             device_id_type=MESH,
         )
 
     def start(step, carry):
-        copy_to(lax.rem(me + step, n), me).start()
-        return carry
-
-    def finish(step, carry):
-        peer = lax.rem(me + n - step, n)
-        copy_to(peer, peer).wait_recv()
-        return carry
-
-    def drain(step, carry):
-        copy_to(lax.rem(me + step, n), me).wait_send()
+        peer = (me + step) & (n - 1)
+        copy(peer, peer, me).start()
         return carry
 
     lax.fori_loop(1, n, start, 0)
     target[pl.ds(me, 1)] = source[pl.ds(me, 1)]
-    lax.fori_loop(1, n, finish, 0)
-    lax.fori_loop(1, n, drain, 0)
+    meanwhile()
+    every = copy((me + 1) & (n - 1), pl.ds(0, n - 1), pl.ds(0, n - 1))
+    every.wait_recv()
+    every.wait_send()
+
+
+def make_bands(mid_high, mid_low, edge_high, edge_low, col_high, col_low):
+    for kernel, sigma in enumerate(SIGMAS):
+        shape = (2 * HALO, 4 * HALO)
+        high, low = split(taps((iota(shape, 1) - iota(shape, 0) - HALO).astype(F32), sigma))
+        for band, mid, edges in ((high, mid_high, edge_high), (low, mid_low, edge_low)):
+            mid[kernel * 2 * HALO : (kernel + 1) * 2 * HALO] = band
+            for e in range(2):
+                edges[e, kernel * HALO : (kernel + 1) * HALO] = band[e * HALO : (e + 1) * HALO]
+        shape = (2 * CHUNK, CHUNK)
+        high, low = split(taps((iota(shape, 0) - iota(shape, 1) - SIDE).astype(F32), sigma))
+        col_high[kernel] = high
+        col_low[kernel] = low
+
+
+BANDS = [
+    jax.ShapeDtypeStruct(shape, BF16)
+    for shape in ((6 * HALO, 4 * HALO), (2, 3 * HALO, 4 * HALO), (3, 2 * CHUNK, CHUNK))
+    for _ in range(2)
+]
 
 
 def route_kernel(
-    n, cols, dose, frac, pos, count, tile, recv, order, parts, ordered, send, send_sem, recv_sem
+    n, cols, dose, frac, pos, count, tile, recv, order, *rest
 ):
+    bands, (parts, ordered, send, send_sem, recv_sem) = rest[:6], rest[6:]
     row, me = lax.axis_index("row"), lax.axis_index("col")
     barrier = greet_all(n, me, row)
     blocks = tile.shape[1]
@@ -166,7 +182,7 @@
     onehot = jnp.where(chosen, 1.0, 0.0).astype(BF16)
     send[...] = dot(onehot, ordered[...].reshape(width, LANES).astype(BF16)).reshape(n, 8, LANES)
     pl.semaphore_wait(barrier, n - 1)
-    exchange(n, me, row, send, recv, send_sem, recv_sem)
+    exchange(n, me, row, send, recv, send_sem, recv_sem, lambda: make_bands(*bands))
 
 
 def route(n, cols, dose, frac, pos, count, tile):
@@ -177,15 +193,16 @@
         out_shape=[
             jax.ShapeDtypeStruct((n, 8, LANES), F32),
             jax.ShapeDtypeStruct((blocks, LANES), I32),
+            *BANDS,
         ],
         in_specs=[vmem] * 5,
-        out_specs=[vmem] * 2,
+        out_specs=[vmem] * 8,
         scratch_shapes=[
             pltpu.VMEM((blocks, 16, LANES), F32),
             pltpu.VMEM((blocks, 16, LANES), F32),
             pltpu.VMEM((n, 8, LANES), F32),
-            pltpu.SemaphoreType.DMA((n,)),
-            pltpu.SemaphoreType.DMA((n,)),
+            pltpu.SemaphoreType.DMA,
+            pltpu.SemaphoreType.DMA,
         ],
         compiler_params=pltpu.CompilerParams(
             collective_id=0, has_side_effects=True, vmem_limit_bytes=8 * 2**20
@@ -204,7 +221,7 @@
     chosen = (placed == 2 * (col >> 3) + (col & 7)) & ((col & 7) < 2)
     onehot = jnp.where(chosen, 1.0, 0.0).astype(BF16)
     pl.semaphore_wait(barrier, n - 1)
-    exchange(n, me, row, grads, back, send_sem, recv_sem)
+    exchange(n, me, row, grads, back, send_sem, recv_sem, lambda: None)
     found = pick(onehot, back[...].reshape(8 * n, LANES))
     out[...] = jnp.take_along_axis(found, order[...], axis=1)
 
@@ -218,8 +235,8 @@
         out_specs=vmem,
         scratch_shapes=[
             pltpu.VMEM((n, 8, LANES), F32),
-            pltpu.SemaphoreType.DMA((n,)),
-            pltpu.SemaphoreType.DMA((n,)),
+            pltpu.SemaphoreType.DMA,
+            pltpu.SemaphoreType.DMA,
         ],
         compiler_params=pltpu.CompilerParams(
             collective_id=2, has_side_effects=True, vmem_limit_bytes=8 * 2**20
@@ -441,8 +458,9 @@
 
 def blur_kernel(
     dims, dose, target_far, zone, zone_weights,
+    mid_high, mid_low, edge_high, edge_low, col_high, col_low,
     exposure, grad_high, grad_low,
-    target, near_sem, mid_high, mid_low, edge_high, edge_low, col_high, col_low,
+    target, near_sem,
     zone_own, zone_in, halo_rows, halo_cols, halo_corners, dose_high, dose_low, part_high, part_low,
     mixed_high, mixed_low, error, weight, sends, recvs, zone_send, zone_recv,
 ):
@@ -541,18 +559,6 @@
         @pl.when(exists(side))
         def _(side=side):
             pl.semaphore_signal(barrier, inc=1, device_id=neighbour(side), device_id_type=MESH)
-
-    for kernel, sigma in enumerate(SIGMAS):
-        shape = (2 * HALO, 4 * HALO)
-        high, low = split(taps((iota(shape, 1) - iota(shape, 0) - HALO).astype(F32), sigma))
-        for band, mid, edges in ((high, mid_high, edge_high), (low, mid_low, edge_low)):
-            mid[kernel * 2 * HALO : (kernel + 1) * 2 * HALO] = band
-            for e in range(2):
-                edges[e, kernel * HALO : (kernel + 1) * HALO] = band[e * HALO : (e + 1) * HALO]
-        shape = (2 * CHUNK, CHUNK)
-        high, low = split(taps((iota(shape, 0) - iota(shape, 1) - SIDE).astype(F32), sigma))
-        col_high[kernel] = high
-        col_low[kernel] = low
 
     tall = 1 + jnp.where(row > 0, 1, 0) + jnp.where(row < n_row - 1, 1, 0)
     broad = 1 + jnp.where(col > 0, 1, 0) + jnp.where(col < n_col - 1, 1, 0)
@@ -700,11 +706,10 @@
     def nothing(u):
         return None
 
-    near.wait()
     await_halo(dose, 0, (8, 9))
     put_dose(halo_cols[0, 0], HALO, 0)
     put_dose(halo_cols[0, 1], HALO, SIDE + cols)
-    sweep(tile_forward, window_forward, 0, nothing, nothing)
+    sweep(tile_forward, window_forward, 0, lambda u: near.wait() if u == 0 else None, nothing)
 
     def arrive(turn, field, put, u):
         chunks = (0, 1, 2) if u == 0 else (u + 2,) if u + 2 < steps else ()
@@ -744,7 +749,7 @@
             zone_copy(side).wait_send()
 
 
-def blur(dims, dose, target, zone, zone_weights):
+def blur(dims, dose, target, zone, zone_weights, bands):
     rows, cols = dose.shape
     wide, high = cols + 2 * SIDE, rows + 2 * HALO
     vmem = pl.BlockSpec(memory_space=pltpu.VMEM)
@@ -757,17 +762,11 @@
             jax.ShapeDtypeStruct((rows, cols), BF16),
             jax.ShapeDtypeStruct((rows, cols), BF16),
         ],
-        in_specs=[vmem, pl.BlockSpec(memory_space=pl.ANY), vmem, smem],
+        in_specs=[vmem, pl.BlockSpec(memory_space=pl.ANY), vmem, smem, *[vmem] * 6],
         out_specs=[vmem] * 3,
         scratch_shapes=[
             pltpu.VMEM((rows, cols), F32),
             dma,
-            pltpu.VMEM((6 * HALO, 4 * HALO), BF16),
-            pltpu.VMEM((6 * HALO, 4 * HALO), BF16),
-            pltpu.VMEM((2, 3 * HALO, 4 * HALO), BF16),
-            pltpu.VMEM((2, 3 * HALO, 4 * HALO), BF16),
-            pltpu.VMEM((3, 2 * CHUNK, CHUNK), BF16),
-            pltpu.VMEM((3, 2 * CHUNK, CHUNK), BF16),
             pltpu.VMEM((8, LANES), I32),
             pltpu.VMEM((8, 8, LANES), I32),
             pltpu.VMEM((2, 2, HALO, cols), F32),
@@ -788,16 +787,16 @@
         ),
         cost_estimate=cost(25),
         name="blur",
-    )(dose, far(target), far(zone), far(zone_weights))
+    )(dose, far(target), far(zone), far(zone_weights), *bands)
 
 
 def per_device(dims, shot_dose, shot_frac, shot_pos, block_count, shot_tile, zone, zone_weights, target):
     n = dims[1]
     rows, cols = target.shape
     count, tile = block_count.reshape(1, -1), shot_tile.reshape(1, -1)
-    recv, order = route(n, cols, shot_dose, shot_frac, shot_pos, count, tile)
+    recv, order, *bands = route(n, cols, shot_dose, shot_frac, shot_pos, count, tile)
     dose, buf, spans = deposit(recv, rows, cols)
-    exposure, grad_high, grad_low = blur(dims, dose, target, zone, zone_weights.T)
+    exposure, grad_high, grad_low = blur(dims, dose, target, zone, zone_weights.T, bands)
     slot_grad, exposure = sample(n, grad_high, grad_low, buf, spans, exposure)
     return exposure, give_back(n, slot_grad, tile, order)
 

time: 63.2 us -> 60.7 us (0.960)
  Pallas kernels: 61.7 us -> 59.3 us
    pallas_call x1, Pallas kernels: 13.7 us -> 10.5 us  [give_back(): pl.pallas_call(functools.partial(return_kernel, n), out_shape=jax.ShapeDt...]
    pallas_call x1, Pallas kernels: 4.39 us -> 5.57 us  [sample(): pl.pallas_call(sample_kernel, out_shape=[jax.ShapeDtypeStruct((n, 8, LANE...]
    pallas_call x1, Pallas kernels: 5.34 us -> 6.44 us  [deposit(): pl.pallas_call(deposit_kernel, out_shape=[jax.ShapeDtypeStruct((rows, col...]
    pallas_call x1, Pallas kernels: 13.9 us -> 12.9 us  [route(): pl.pallas_call(functools.partial(route_kernel, n, cols), out_shape=[jax.S...]
    pallas_call x1, Pallas kernels: 24.4 us -> 23.8 us  [blur(): pl.pallas_call(functools.partial(blur_kernel, dims), out_shape=[jax.Shape...]
where the time goes in v4:
time: 60.7 us; the launch traced here: 60.5 us
  Pallas kernels  59.3 us (98%)
  between operations  0.67 us (1%)
  local copies, waits for them, and re-layouts  0.61 us (1%)
    pallas_call x1, Pallas kernels, blur(): pl.pallas_call(functools.partial(blur_kernel, dims), out_shape=[jax.Shape...  23.8 us
    pallas_call x1, Pallas kernels, route(): pl.pallas_call(functools.partial(route_kernel, n, cols), out_shape=[jax.S...  12.9 us
    pallas_call x1, Pallas kernels, give_back(): pl.pallas_call(functools.partial(return_kernel, n), out_shape=jax.ShapeDt...  10.5 us
    pallas_call x1, Pallas kernels, deposit(): pl.pallas_call(deposit_kernel, out_shape=[jax.ShapeDtypeStruct((rows, col...  6.44 us
    pallas_call x1, Pallas kernels, sample(): pl.pallas_call(sample_kernel, out_shape=[jax.ShapeDtypeStruct((n, 8, LANE...  5.57 us

profile of v4, /device:TPU:1, one launch (start us, length us, event | category | flops | bytes accessed | tf_op | source)
XLA Modules:
  0.0 60.5 jit_solution(8001964318683294723)
XLA Ops:
  0.6 12.9 %route.1 = (f32[32,8,128]{2,1,0:T(8,128)S(1)}, s32[32,128]{1,0:T(8,128)S(1)}, bf16[384,256]{1,0:T(8,128)(2,1)S(1)}, bf16[384,256]{1,0:T(8,128)(2,1)S(1)}, bf16[2...) custom-call(f32[32,128]{1,0:T(8,128)} %dose.1, ...), custom_call_target="tpu_custom_call" | custom-call | bytes 30000000 | tf_op jit(solution)/shard_map/route/pallas_call | solution.py:191
  13.6 6.4 %deposit.1 = (f32[256,1024]{1,0:T(8,128)S(1)}, f32[264,8,128]{2,1,0:T(8,128)S(1)}, s32[8,128]{1,0:T(8,128)S(1)}) custom-call(f32[32,8,128]{2,1,0:T(8,128)S(1)} %get-tuple-element.18.recv), custom_call_target="tpu_custom_call" | custom-call | bytes 24000000 | tf_op jit(solution)/shard_map/deposit/pallas_call | solution.py:358
  20.0 23.8 %blur.1 = (f32[256,1024]{1,0:T(8,128)S(1)}, bf16[256,1024]{1,0:T(8,128)(2,1)S(1)}, bf16[256,1024]{1,0:T(8,128)(2,1)S(1)}) custom-call(f32[256,1024]{1,0:T(8,128)S(1)} %get-tuple-element.19.dose, f32[256,1024]{1,0:T(8,128)} %target_far.1, s32[4,16]{1,0:T(4,128)} %zone.1, f32[3,8]{1,0:T(4,128)} %bitcast.3, bf16[384,256]{1,0:T(8,128)(2,1)S(1)} %get-tuple-element.20.mid_high, ...), custom_call_target="tpu_custom_call" | custom-call | bytes 75000000 | tf_op jit(solution)/shard_map/blur/pallas_call | solution.py:758
  43.8 5.6 %sample.1 = (f32[32,8,128]{2,1,0:T(8,128)S(1)}, f32[256,1024]{1,0:T(8,128)}) custom-call(bf16[256,1024]{1,0:T(8,128)(2,1)S(1)} %get-tuple-element.26.grad_high, bf16[256,1024]{1,0:T(8,128)(2,1)S(1)} %get-tuple-element.27.grad_low, f32[264,8,128]{2,1,0:T(8,128)S(1)} %get-tuple-element.28.buf, s32[8,128]{1,0:T(8,128)S(1)} %get-tuple-element.29.spans, ...), custom_call_target="tpu_custom_call" | custom-call | bytes 24000000 | tf_op jit(solution)/shard_map/sample/pallas_call | solution.py:439
  49.4 10.5 %give_back.1 = f32[32,128]{1,0:T(8,128)S(1)} custom-call(f32[32,8,128]{2,1,0:T(8,128)S(1)} %get-tuple-element.32.grads, s32[1,32]{1,0:T(1,128)} %bitcast.5, s32[32,128]{1,0:T(8,128)S(1)} %get-tuple-element.33.order), custom_call_target="tpu_custom_call" | custom-call | bytes 30000000 | tf_op jit(solution)/shard_map/give_back/pallas_call | solution.py:231
  59.9 0.6 %copy.11 = f32[32,128]{1,0:T(8,128)} copy(f32[32,128]{1,0:T(8,128)S(1)} %give_back.1) | data formatting | bytes 32768

commit v5 on v4

--- a/solution.py
+++ b/solution.py
@@ -84,13 +84,9 @@
 
 def greet_all(n, me, row):
     barrier = pltpu.get_barrier_semaphore()
-
-    def greet(step, carry):
+    for step in range(1, n):
         peer = (me + step) & (n - 1)
         pl.semaphore_signal(barrier, inc=1, device_id=(row, peer), device_id_type=MESH)
-        return carry
-
-    lax.fori_loop(1, n, greet, 0)
     return barrier
 
 
@@ -105,12 +101,9 @@
             device_id_type=MESH,
         )
 
-    def start(step, carry):
+    for step in range(1, n):
         peer = (me + step) & (n - 1)
         copy(peer, peer, me).start()
-        return carry
-
-    lax.fori_loop(1, n, start, 0)
     target[pl.ds(me, 1)] = source[pl.ds(me, 1)]
     meanwhile()
     every = copy((me + 1) & (n - 1), pl.ds(0, n - 1), pl.ds(0, n - 1))
@@ -217,12 +210,10 @@
     barrier = greet_all(n, me, row)
     blocks = tile.shape[1]
     placed, _ = slots_of(upright(tile[...]), blocks)
-    col = iota((blocks, 8 * n), 1)
-    chosen = (placed == 2 * (col >> 3) + (col & 7)) & ((col & 7) < 2)
-    onehot = jnp.where(chosen, 1.0, 0.0).astype(BF16)
+    onehot = jnp.where(placed == iota((blocks, 2 * n), 1), 1.0, 0.0).astype(BF16)
     pl.semaphore_wait(barrier, n - 1)
     exchange(n, me, row, grads, back, send_sem, recv_sem, lambda: None)
-    found = pick(onehot, back[...].reshape(8 * n, LANES))
+    found = pick(onehot, jnp.concatenate([back[i] for i in range(n)], axis=0))
     out[...] = jnp.take_along_axis(found, order[...], axis=1)
 
 
@@ -234,7 +225,7 @@
         in_specs=[vmem] * 3,
         out_specs=vmem,
         scratch_shapes=[
-            pltpu.VMEM((n, 8, LANES), F32),
+            pltpu.VMEM((n, 2, LANES), F32),
             pltpu.SemaphoreType.DMA,
             pltpu.SemaphoreType.DMA,
         ],
@@ -403,7 +394,7 @@
 
     lax.fori_loop(0, spans[0, LANES - 1], sample, 0)
 
-    lane, row = iota((1, LANES), 1), iota((8, LANES), 0)
+    lane = iota((1, LANES), 1)
 
     def take(begin, amount, at):
         lane_at, tile_at = at & (LANES - 1), at >> 7
@@ -426,7 +417,7 @@
                 total = total + take(begin, amount, at[q])
                 at[q] = at[q] + amount
             both.append(total)
-        out[i] = jnp.where(row == 0, both[0], jnp.where(row == 1, both[1], 0.0))
+        out[i] = jnp.concatenate(both, axis=0)
         return at
 
     lax.fori_loop(0, n // 8, spread, [jnp.int32(s * LANES) for s in starts])
@@ -439,7 +430,7 @@
     return pl.pallas_call(
         sample_kernel,
         out_shape=[
-            jax.ShapeDtypeStruct((n, 8, LANES), F32),
+            jax.ShapeDtypeStruct((n, 2, LANES), F32),
             jax.ShapeDtypeStruct(exposure.shape, F32),
         ],
         in_specs=[vmem, vmem, vmem, smem, pl.BlockSpec(memory_space=pl.ANY)],
@@ -536,9 +527,15 @@
     def await_halo(field, turn, pieces):
         by_side(pieces, lambda piece: halo_copy(field, turn, OPPOSITE[piece]).wait_recv())
 
+    barrier = pltpu.get_barrier_semaphore()
+    for side in range(8):
+
+        @pl.when(exists(side))
+        def _(side=side):
+            pl.semaphore_signal(barrier, inc=1, device_id=neighbour(side), device_id_type=MESH)
+
     near = pltpu.make_async_copy(target_far, target, near_sem)
     near.start()
-    barrier = pltpu.get_barrier_semaphore()
     zone_own[...] = jnp.zeros_like(zone_own)
     zone_own[0 : zone.shape[0], 0 : zone.shape[1]] = zone[...]
     for side in range(8):
@@ -553,12 +550,6 @@
                 else:
                     halo_corners[turn, side - 4] = jnp.zeros((HALO, SIDE), F32)
             zone_in[side] = jnp.zeros_like(zone_own)
-
-    for side in range(8):
-
-        @pl.when(exists(side))
-        def _(side=side):
-            pl.semaphore_signal(barrier, inc=1, device_id=neighbour(side), device_id_type=MESH)
 
     tall = 1 + jnp.where(row > 0, 1, 0) + jnp.where(row < n_row - 1, 1, 0)
     broad = 1 + jnp.where(col > 0, 1, 0) + jnp.where(col < n_col - 1, 1, 0)

time: 60.7 us -> 61.1 us (level)
    pallas_call x1, Pallas kernels: 10.5 us -> 12.4 us  [give_back(): pl.pallas_call(functools.partial(return_kernel, n), out_shape=jax.ShapeDt...]
    pallas_call x1, Pallas kernels: 5.57 us -> 4.4 us  [sample(): pl.pallas_call(sample_kernel, out_shape=[jax.ShapeDtypeStruct((n, 2, LANE...]
    pallas_call x1, Pallas kernels: 6.44 us -> 5.33 us  [deposit(): pl.pallas_call(deposit_kernel, out_shape=[jax.ShapeDtypeStruct((rows, col...]
    pallas_call x1, Pallas kernels: 23.8 us -> 24.6 us  [blur(): pl.pallas_call(functools.partial(blur_kernel, dims), out_shape=[jax.Shape...]
where the time goes in v5:
time: 61.1 us; the launch traced here: 60.9 us
  Pallas kernels  59.6 us (98%)
  between operations  0.67 us (1%)
    pallas_call x1, Pallas kernels, blur(): pl.pallas_call(functools.partial(blur_kernel, dims), out_shape=[jax.Shape...  24.6 us
    pallas_call x1, Pallas kernels, route(): pl.pallas_call(functools.partial(route_kernel, n, cols), out_shape=[jax.S...  12.9 us
    pallas_call x1, Pallas kernels, give_back(): pl.pallas_call(functools.partial(return_kernel, n), out_shape=jax.ShapeDt...  12.4 us
    pallas_call x1, Pallas kernels, deposit(): pl.pallas_call(deposit_kernel, out_shape=[jax.ShapeDtypeStruct((rows, col...  5.33 us
    pallas_call x1, Pallas kernels, sample(): pl.pallas_call(sample_kernel, out_shape=[jax.ShapeDtypeStruct((n, 2, LANE...  4.4 us

profile of v5, /device:TPU:1, one launch (start us, length us, event | category | flops | bytes accessed | tf_op | source)
XLA Modules:
  0.0 60.9 jit_solution(7129228541278426195)
XLA Ops:
  0.6 12.9 %route.1 = (f32[32,8,128]{2,1,0:T(8,128)S(1)}, s32[32,128]{1,0:T(8,128)S(1)}, bf16[384,256]{1,0:T(8,128)(2,1)S(1)}, bf16[384,256]{1,0:T(8,128)(2,1)S(1)}, bf16[2...) custom-call(f32[32,128]{1,0:T(8,128)} %dose.1, ...), custom_call_target="tpu_custom_call" | custom-call | bytes 30000000 | tf_op jit(solution)/shard_map/route/pallas_call | solution.py:184
  13.5 5.3 %deposit.1 = (f32[256,1024]{1,0:T(8,128)S(1)}, f32[264,8,128]{2,1,0:T(8,128)S(1)}, s32[8,128]{1,0:T(8,128)S(1)}) custom-call(f32[32,8,128]{2,1,0:T(8,128)S(1)} %get-tuple-element.18.recv), custom_call_target="tpu_custom_call" | custom-call | bytes 24000000 | tf_op jit(solution)/shard_map/deposit/pallas_call | solution.py:349
  18.9 24.6 %blur.1 = (f32[256,1024]{1,0:T(8,128)S(1)}, bf16[256,1024]{1,0:T(8,128)(2,1)S(1)}, bf16[256,1024]{1,0:T(8,128)(2,1)S(1)}) custom-call(f32[256,1024]{1,0:T(8,128)S(1)} %get-tuple-element.19.dose, f32[256,1024]{1,0:T(8,128)} %target_far.1, s32[4,16]{1,0:T(4,128)} %zone.1, f32[3,8]{1,0:T(4,128)} %bitcast.3, bf16[384,256]{1,0:T(8,128)(2,1)S(1)} %get-tuple-element.20.mid_high, ...), custom_call_target="tpu_custom_call" | custom-call | bytes 75000000 | tf_op jit(solution)/shard_map/blur/pallas_call | solution.py:749
  43.5 4.4 %sample.1 = (f32[32,2,128]{2,1,0:T(2,128)S(1)}, f32[256,1024]{1,0:T(8,128)}) custom-call(bf16[256,1024]{1,0:T(8,128)(2,1)S(1)} %get-tuple-element.26.grad_high, bf16[256,1024]{1,0:T(8,128)(2,1)S(1)} %get-tuple-element.27.grad_low, f32[264,8,128]{2,1,0:T(8,128)S(1)} %get-tuple-element.28.buf, s32[8,128]{1,0:T(8,128)S(1)} %get-tuple-element.29.spans, ...), custom_call_target="tpu_custom_call" | custom-call | bytes 24000000 | tf_op jit(solution)/shard_map/sample/pallas_call | solution.py:430
  47.9 12.4 %give_back.1 = f32[32,128]{1,0:T(8,128)S(1)} custom-call(f32[32,2,128]{2,1,0:T(2,128)S(1)} %get-tuple-element.32.grads, s32[1,32]{1,0:T(1,128)} %bitcast.5, s32[32,128]{1,0:T(8,128)S(1)} %get-tuple-element.33.order), custom_call_target="tpu_custom_call" | custom-call | bytes 30000000 | tf_op jit(solution)/shard_map/give_back/pallas_call | solution.py:222
  60.3 0.6 copy.11

commit v6 on v5

--- a/solution.py
+++ b/solution.py
@@ -683,8 +683,7 @@
         weight[...] = dot(piece, spread) if _ == 0 else weight[...] + dot(piece, spread)
         table = table - piece.astype(F32)
 
-    def sweep(tile, window, edges, before, after):
-        ahead = 2
+    def sweep(tile, window, edges, before, after, ahead=2):
         done = 0
         for u in range(steps):
             before(u)
@@ -702,16 +701,16 @@
     put_dose(halo_cols[0, 1], HALO, SIDE + cols)
     sweep(tile_forward, window_forward, 0, lambda u: near.wait() if u == 0 else None, nothing)
 
-    def arrive(turn, field, put, u):
-        chunks = (0, 1, 2) if u == 0 else (u + 2,) if u + 2 < steps else ()
-        corners = (10, 12) if u == 0 else (11, 13) if u == steps - 2 else ()
+    def arrive(turn, field, put, ahead, u):
+        chunks = tuple(range(ahead + 1)) if u == 0 else (u + ahead,) if u + ahead < steps else ()
+        corners = (10, 12) if u == 0 else (11, 13) if u == steps - ahead else ()
         await_halo(field, turn, (*chunks, *(4 + c for c in chunks), *corners))
         for side, square in ((0, 0), (1, rows // HALO + 1)):
             for c in chunks:
                 put(halo_rows[turn, side, :, c * CHUNK : (c + 1) * CHUNK], square, SIDE + c * CHUNK)
             if u == 0:
                 put(halo_corners[turn, 2 * side], square, 0)
-            if u == steps - 2:
+            if u == steps - ahead:
                 put(halo_corners[turn, 2 * side + 1], square, SIDE + cols)
 
     def send_error(u):
@@ -722,15 +721,16 @@
         tile_forward,
         window_forward,
         1,
-        lambda u: arrive(0, dose, lambda value, square, at: put_dose(value, square * HALO, at), u),
+        lambda u: arrive(0, dose, lambda value, square, at: put_dose(value, square * HALO, at), 1, u),
         send_error,
+        ahead=1,
     )
     await_halo(error, 1, (8, 9))
     for side, at in ((0, 0), (1, SIDE + cols)):
         for square in range(rows // HALO):
             put_part(halo_cols[1, side, square * HALO : (square + 1) * HALO], 1 + square, at)
     sweep(tile_backward, window_backward, 0, nothing, nothing)
-    sweep(tile_backward, window_backward, 1, lambda u: arrive(1, error, put_part, u), nothing)
+    sweep(tile_backward, window_backward, 1, lambda u: arrive(1, error, put_part, 2, u), nothing)
     by_side(range(14), lambda piece: halo_copy(dose, 0, piece).wait_send())
     by_side(range(14), lambda piece: halo_copy(error, 1, piece).wait_send())
     for side in range(8):

time: 61.1 us -> 60 us (0.982)
  Pallas kernels: 59.6 us -> 58.5 us
    pallas_call x1, Pallas kernels: 24.6 us -> 23.4 us  [blur(): pl.pallas_call(functools.partial(blur_kernel, dims), out_shape=[jax.Shape...]
where the time goes in v6:
time: 60 us; the launch traced here: 59.8 us
  Pallas kernels  58.5 us (98%)
  between operations  0.67 us (1%)
  local copies, waits for them, and re-layouts  0.61 us (1%)
    pallas_call x1, Pallas kernels, blur(): pl.pallas_call(functools.partial(blur_kernel, dims), out_shape=[jax.Shape...  23.4 us
    pallas_call x1, Pallas kernels, route(): pl.pallas_call(functools.partial(route_kernel, n, cols), out_shape=[jax.S...  12.9 us
    pallas_call x1, Pallas kernels, give_back(): pl.pallas_call(functools.partial(return_kernel, n), out_shape=jax.ShapeDt...  12.4 us
    pallas_call x1, Pallas kernels, deposit(): pl.pallas_call(deposit_kernel, out_shape=[jax.ShapeDtypeStruct((rows, col...  5.33 us
    pallas_call x1, Pallas kernels, sample(): pl.pallas_call(sample_kernel, out_shape=[jax.ShapeDtypeStruct((n, 2, LANE...  4.4 us

profile of v6, /device:TPU:1, one launch (start us, length us, event | category | flops | bytes accessed | tf_op | source)
XLA Modules:
  0.0 59.8 jit_solution(2692361336217768213)
XLA Ops:
  0.6 12.9 %route.1 = (f32[32,8,128]{2,1,0:T(8,128)S(1)}, s32[32,128]{1,0:T(8,128)S(1)}, bf16[384,256]{1,0:T(8,128)(2,1)S(1)}, bf16[384,256]{1,0:T(8,128)(2,1)S(1)}, bf16[2...) custom-call(f32[32,128]{1,0:T(8,128)} %dose.1, ...), custom_call_target="tpu_custom_call" | custom-call | bytes 30000000 | tf_op jit(solution)/shard_map/route/pallas_call | solution.py:184
  13.5 5.3 %deposit.1 = (f32[256,1024]{1,0:T(8,128)S(1)}, f32[264,8,128]{2,1,0:T(8,128)S(1)}, s32[8,128]{1,0:T(8,128)S(1)}) custom-call(f32[32,8,128]{2,1,0:T(8,128)S(1)} %get-tuple-element.18.recv), custom_call_target="tpu_custom_call" | custom-call | bytes 24000000 | tf_op jit(solution)/shard_map/deposit/pallas_call | solution.py:349
  18.9 23.4 %blur.1 = (f32[256,1024]{1,0:T(8,128)S(1)}, bf16[256,1024]{1,0:T(8,128)(2,1)S(1)}, bf16[256,1024]{1,0:T(8,128)(2,1)S(1)}) custom-call(f32[256,1024]{1,0:T(8,128)S(1)} %get-tuple-element.19.dose, f32[256,1024]{1,0:T(8,128)} %target_far.1, s32[4,16]{1,0:T(4,128)} %zone.1, f32[3,8]{1,0:T(4,128)} %bitcast.3, bf16[384,256]{1,0:T(8,128)(2,1)S(1)} %get-tuple-element.20.mid_high, ...), custom_call_target="tpu_custom_call" | custom-call | bytes 75000000 | tf_op jit(solution)/shard_map/blur/pallas_call | solution.py:749
  42.3 4.4 %sample.1 = (f32[32,2,128]{2,1,0:T(2,128)S(1)}, f32[256,1024]{1,0:T(8,128)}) custom-call(bf16[256,1024]{1,0:T(8,128)(2,1)S(1)} %get-tuple-element.26.grad_high, bf16[256,1024]{1,0:T(8,128)(2,1)S(1)} %get-tuple-element.27.grad_low, f32[264,8,128]{2,1,0:T(8,128)S(1)} %get-tuple-element.28.buf, s32[8,128]{1,0:T(8,128)S(1)} %get-tuple-element.29.spans, ...), custom_call_target="tpu_custom_call" | custom-call | bytes 24000000 | tf_op jit(solution)/shard_map/sample/pallas_call | solution.py:430
  46.7 12.4 %give_back.1 = f32[32,128]{1,0:T(8,128)S(1)} custom-call(f32[32,2,128]{2,1,0:T(2,128)S(1)} %get-tuple-element.32.grads, s32[1,32]{1,0:T(1,128)} %bitcast.5, s32[32,128]{1,0:T(8,128)S(1)} %get-tuple-element.33.order), custom_call_target="tpu_custom_call" | custom-call | bytes 30000000 | tf_op jit(solution)/shard_map/give_back/pallas_call | solution.py:222
  59.1 0.6 %copy.11 = f32[32,128]{1,0:T(8,128)} copy(f32[32,128]{1,0:T(8,128)S(1)} %give_back.1) | data formatting | bytes 32768

commit v7 on v6

--- a/solution.py
+++ b/solution.py
@@ -730,7 +730,7 @@
         for square in range(rows // HALO):
             put_part(halo_cols[1, side, square * HALO : (square + 1) * HALO], 1 + square, at)
     sweep(tile_backward, window_backward, 0, nothing, nothing)
-    sweep(tile_backward, window_backward, 1, lambda u: arrive(1, error, put_part, 2, u), nothing)
+    sweep(tile_backward, window_backward, 1, lambda u: arrive(1, error, put_part, 1, u), nothing, 1)
     by_side(range(14), lambda piece: halo_copy(dose, 0, piece).wait_send())
     by_side(range(14), lambda piece: halo_copy(error, 1, piece).wait_send())
     for side in range(8):

time: 60 us -> 60.9 us (1.015)
  no operation moved by 1% of the time
where the time goes in v7:
time: 60.9 us; the launch traced here: 60.4 us
  Pallas kernels  59.1 us (97%)
  between operations  0.67 us (1%)
  local copies, waits for them, and re-layouts  0.61 us (1%)
    pallas_call x1, Pallas kernels, blur(): pl.pallas_call(functools.partial(blur_kernel, dims), out_shape=[jax.Shape...  23.9 us
    pallas_call x1, Pallas kernels, route(): pl.pallas_call(functools.partial(route_kernel, n, cols), out_shape=[jax.S...  12.9 us
    pallas_call x1, Pallas kernels, give_back(): pl.pallas_call(functools.partial(return_kernel, n), out_shape=jax.ShapeDt...  12.6 us
    pallas_call x1, Pallas kernels, deposit(): pl.pallas_call(deposit_kernel, out_shape=[jax.ShapeDtypeStruct((rows, col...  5.33 us
    pallas_call x1, Pallas kernels, sample(): pl.pallas_call(sample_kernel, out_shape=[jax.ShapeDtypeStruct((n, 2, LANE...  4.4 us

profile of v7, /device:TPU:1, one launch (start us, length us, event | category | flops | bytes accessed | tf_op | source)
XLA Modules:
  0.0 60.4 jit_solution(5803652559409088547)
XLA Ops:
  0.6 12.9 %route.1 = (f32[32,8,128]{2,1,0:T(8,128)S(1)}, s32[32,128]{1,0:T(8,128)S(1)}, bf16[384,256]{1,0:T(8,128)(2,1)S(1)}, bf16[384,256]{1,0:T(8,128)(2,1)S(1)}, bf16[2...) custom-call(f32[32,128]{1,0:T(8,128)} %dose.1, ...), custom_call_target="tpu_custom_call" | custom-call | bytes 30000000 | tf_op jit(solution)/shard_map/route/pallas_call | solution.py:184
  13.5 5.3 %deposit.1 = (f32[256,1024]{1,0:T(8,128)S(1)}, f32[264,8,128]{2,1,0:T(8,128)S(1)}, s32[8,128]{1,0:T(8,128)S(1)}) custom-call(f32[32,8,128]{2,1,0:T(8,128)S(1)} %get-tuple-element.18.recv), custom_call_target="tpu_custom_call" | custom-call | bytes 24000000 | tf_op jit(solution)/shard_map/deposit/pallas_call | solution.py:349
  18.9 23.9 %blur.1 = (f32[256,1024]{1,0:T(8,128)S(1)}, bf16[256,1024]{1,0:T(8,128)(2,1)S(1)}, bf16[256,1024]{1,0:T(8,128)(2,1)S(1)}) custom-call(f32[256,1024]{1,0:T(8,128)S(1)} %get-tuple-element.19.dose, f32[256,1024]{1,0:T(8,128)} %target_far.1, s32[4,16]{1,0:T(4,128)} %zone.1, f32[3,8]{1,0:T(4,128)} %bitcast.3, bf16[384,256]{1,0:T(8,128)(2,1)S(1)} %get-tuple-element.20.mid_high, ...), custom_call_target="tpu_custom_call" | custom-call | bytes 75000000 | tf_op jit(solution)/shard_map/blur/pallas_call | solution.py:749
  42.8 4.4 %sample.1 = (f32[32,2,128]{2,1,0:T(2,128)S(1)}, f32[256,1024]{1,0:T(8,128)}) custom-call(bf16[256,1024]{1,0:T(8,128)(2,1)S(1)} %get-tuple-element.26.grad_high, bf16[256,1024]{1,0:T(8,128)(2,1)S(1)} %get-tuple-element.27.grad_low, f32[264,8,128]{2,1,0:T(8,128)S(1)} %get-tuple-element.28.buf, s32[8,128]{1,0:T(8,128)S(1)} %get-tuple-element.29.spans, ...), custom_call_target="tpu_custom_call" | custom-call | bytes 24000000 | tf_op jit(solution)/shard_map/sample/pallas_call | solution.py:430
  47.2 12.6 %give_back.1 = f32[32,128]{1,0:T(8,128)S(1)} custom-call(f32[32,2,128]{2,1,0:T(2,128)S(1)} %get-tuple-element.32.grads, s32[1,32]{1,0:T(1,128)} %bitcast.5, s32[32,128]{1,0:T(8,128)S(1)} %get-tuple-element.33.order), custom_call_target="tpu_custom_call" | custom-call | bytes 30000000 | tf_op jit(solution)/shard_map/give_back/pallas_call | solution.py:222
  59.8 0.6 %copy.11 = f32[32,128]{1,0:T(8,128)} copy(f32[32,128]{1,0:T(8,128)S(1)} %give_back.1) | data formatting | bytes 32768
